TPU v7x, 32 devices: a whole 2x2x4 slice. The times are simulated.
32 devices in a mesh: dp: 16 (over z, y, x), seq: 2 (over core).
Axes of the slice: x: 2, y: 2, z: 4, core: 2. Of those that a mesh axis runs over, the one named last changes fastest.
Arguments:
- tokens: bfloat16 [16, 2048, 768], P('dp', 'seq'), may hold values from -6 to 6
- lengths: int32 [16, 16], P('dp'), may hold values from 1 to 512, as said below
- partners: int32 [256], replicated, may hold values from 0 to 255, as said below
- query_proj: bfloat16 [768, 768], replicated, may hold values from -0.21875 to 0.21875
- query_bias: float32 [768], replicated, may hold values from -1.25 to 1.25
- key_proj: bfloat16 [768, 768], replicated, may hold values from -0.21875 to 0.21875
- value_proj: bfloat16 [768, 768], replicated, may hold values from -0.21875 to 0.21875
- value_bias: float32 [768], replicated, may hold values from -1.25 to 1.25
- output_proj: bfloat16 [768, 768], replicated, may hold values from -0.875 to 0.875
- output_bias: float32 [768], replicated, may hold values from -1.25 to 1.25
- first_gain: float32 [768], replicated, may hold values from 0.5 to 1.5
- first_shift: float32 [768], replicated, may hold values from -0.3125 to 0.3125
- expand_proj: bfloat16 [768, 3072], replicated, may hold values from -0.21875 to 0.21875
- expand_bias: float32 [3072], replicated, may hold values from -1.25 to 1.25
- shrink_proj: bfloat16 [3072, 768], replicated, may hold values from -0.21875 to 0.21875
- shrink_bias: float32 [768], replicated, may hold values from -1.25 to 1.25
- second_gain: float32 [768], replicated, may hold values from 0.5 to 1.5
- second_shift: float32 [768], replicated, may hold values from -0.3125 to 0.3125
Outputs:
- passage_loss: float32 [256], P('dp')
- tokens_grad: float32 [16, 2048, 768], P('dp', 'seq')
- query_proj_grad: float32 [768, 768], replicated
- query_bias_grad: float32 [768], replicated
- key_proj_grad: float32 [768, 768], replicated
- value_projection_gradient: float32 [768, 768], replicated
- value_bias_gradient: float32 [768], replicated
- output_proj_grad: float32 [768, 768], replicated
- output_bias_grad: float32 [768], replicated
- first_gain_grad: float32 [768], replicated
- first_shift_grad: float32 [768], replicated
- expand_proj_grad: float32 [768, 3072], replicated
- expand_bias_grad: float32 [3072], replicated
- shrink_proj_grad: float32 [3072, 768], replicated
- shrink_bias_grad: float32 [768], replicated
- second_gain_grad: float32 [768], replicated
- second_shift_grad: float32 [768], replicated
Inputs may be any that keep to these rules, and one draw needn't show every extreme that they name: `lengths`: in every row exactly one passage has 512 positions and it holds positions 1023 and 1024 of the row; the passages of a row together take at most 2048 positions. `partners`: never the passage itself.
All inputs are finite; a program needn't handle non-finite values.
Results may differ from a plain program's by a relative error of at most 0.015.
Values may be sent and summed in bfloat16 or wider, within the bound.
No kernel may reach another device: no remote copies, remote signals or barrier semaphores. Data moves between devices by JAX's collectives and lax.ppermute only.
A program may use at most 192 MiB of HBM per device.

v0:
```python
import math

import jax
import jax.numpy as jnp
from jax import lax
from jax.sharding import PartitionSpec as P

HEADS = 12


EPS_NORM = 1e-12
BIG_NEG = -1000000000.0
HIGH = lax.Precision.HIGHEST


def layer_norm(resid, gain, shift):
    center = resid - jnp.mean(resid, -1, keepdims=True)
    spread = jnp.mean(center * center, -1, keepdims=True)
    return center * lax.rsqrt(spread + EPS_NORM) * gain + shift


def normalize_rows(pooled):
    return pooled * lax.rsqrt(jnp.sum(pooled * pooled, -1, keepdims=True) + 1e-06)


def gelu_exact(values_in):
    return jax.nn.gelu(values_in, approximate=False)


def to_units(array):
    row_count, length, features = array.shape
    head_size = features // HEADS
    split = array.reshape(row_count, length, HEADS, head_size).transpose(0, 2, 1, 3)
    return split.reshape(row_count * HEADS, length, head_size)


def from_units(array):
    units, length, head_size = array.shape
    row_count = units // HEADS
    joined = array.reshape(row_count, HEADS, length, head_size).transpose(0, 2, 1, 3)
    return joined.reshape(row_count, length, HEADS * head_size)


def score_block(query_block, key_unit, query_seg, key_seg):
    scores = (
        jnp.einsum("qe,ke->qk", query_block, key_unit, preferred_element_type=jnp.float32) * 0.125
    )
    return jnp.where(query_seg[:, None] == key_seg[None, :], scores, BIG_NEG)


def contrast(unit_own, every_unit, own_ids, own_partners):
    columns = jnp.arange(every_unit.shape[0], dtype=jnp.int32)
    scores = jnp.dot(unit_own, every_unit.T, precision=HIGH) * 100.0
    scores = jnp.where(own_ids[:, None] == columns[None, :], BIG_NEG, scores)
    log_sums = jax.scipy.special.logsumexp(scores, -1)
    target = columns[None, :] == own_partners[:, None]
    picked = jnp.sum(jnp.where(target, scores, 0.0), -1)
    weights_soft = jnp.exp(scores - log_sums[:, None]) - target.astype(jnp.float32)
    return (log_sums - picked, weights_soft)


def body(
    tokens,
    lengths,
    partners,
    query_proj,
    query_bias,
    key_proj,
    value_proj,
    value_bias,
    output_proj,
    output_bias,
    first_gain,
    first_shift,
    expand_proj,
    expand_bias,
    shrink_proj,
    shrink_bias,
    second_gain,
    second_shift,
):
    row_count, local_len, features = tokens.shape
    head_size = features // HEADS
    pass_count = lengths.shape[1]
    own_count = row_count * pass_count
    full_len = local_len * lax.axis_size("seq")
    token_start = lax.axis_index("seq") * local_len
    passage_start = lax.axis_index("dp") * own_count
    block = math.gcd(local_len, 512)
    flat_rows = tokens.reshape(row_count * local_len, features)
    flat_wide = flat_rows.astype(jnp.float32)
    ends = jnp.cumsum(lengths, 1)
    positions = jnp.arange(full_len, dtype=jnp.int32)
    segment_full = jnp.sum((positions[None, :, None] >= ends[:, None, :]).astype(jnp.int32), -1)
    segment_here = lax.dynamic_slice_in_dim(segment_full, token_start, local_len, 1)
    members = (
        segment_here[:, None, :] == jnp.arange(pass_count, dtype=jnp.int32)[None, :, None]
    ).astype(jnp.float32)
    lengths_wide = lengths.reshape(own_count, 1).astype(jnp.float32)
    query_segs = jnp.repeat(segment_here, HEADS, 0)
    key_segs = jnp.repeat(segment_full, HEADS, 0)

    def unit_forward(packed):
        query_unit, key_unit, value_unit, query_seg, key_seg = packed

        def one_block(pair):
            query_block, seg_block = pair
            scores = score_block(query_block, key_unit, seg_block, key_seg)
            row_max = jnp.max(scores, -1, keepdims=True)
            shifted = jnp.exp(scores - row_max)
            exp_total = jnp.sum(shifted, -1, keepdims=True)
            probs = (shifted / exp_total).astype(jnp.bfloat16)
            context = jnp.dot(probs, value_unit, preferred_element_type=jnp.float32).astype(
                jnp.bfloat16
            )
            return (context, (row_max + jnp.log(exp_total))[:, 0])

        context, log_total = lax.map(
            one_block, (query_unit.reshape(-1, block, head_size), query_seg.reshape(-1, block))
        )
        return (context.reshape(-1, head_size), log_total.reshape(-1))

    def unit_back(packed):
        query_unit, key_unit, value_unit, query_seg, key_seg, log_unit, grad_unit = packed

        def step(carry, pieces):
            key_acc, value_acc = carry
            query_block, seg_block, log_block, grad_block = pieces
            scores = score_block(query_block, key_unit, seg_block, key_seg)
            probs = jnp.exp(scores - log_block[:, None])
            probability_grad = jnp.einsum(
                "qe,ke->qk", grad_block, value_unit, preferred_element_type=jnp.float32
            )
            inner_sum = jnp.sum(probs * probability_grad, -1, keepdims=True)
            grad_scores = (probs * (probability_grad - inner_sum)).astype(jnp.bfloat16)
            grad_query = (
                jnp.dot(grad_scores, key_unit, preferred_element_type=jnp.float32) * 0.125
            ).astype(jnp.bfloat16)
            key_acc = (
                key_acc
                + jnp.einsum(
                    "qk,qe->ke", grad_scores, query_block, preferred_element_type=jnp.float32
                )
                * 0.125
            )
            value_acc = value_acc + jnp.einsum(
                "qk,qe->ke",
                probs.astype(jnp.bfloat16),
                grad_block,
                preferred_element_type=jnp.float32,
            )
            return ((key_acc, value_acc), grad_query)

        empty = jnp.zeros(key_unit.shape, jnp.float32)
        (key_acc, value_acc), grad_query = lax.scan(
            step,
            (empty, empty),
            (
                query_unit.reshape(-1, block, head_size),
                query_seg.reshape(-1, block),
                log_unit.reshape(-1, block),
                grad_unit.reshape(-1, block, head_size),
            ),
        )
        return (grad_query.reshape(-1, head_size), key_acc, value_acc)

    queries = (
        jnp.dot(flat_rows, query_proj, preferred_element_type=jnp.float32) + query_bias
    ).astype(jnp.bfloat16)
    query_units = to_units(queries.reshape(row_count, local_len, features))
    key_low = jnp.dot(flat_rows, key_proj, preferred_element_type=jnp.float32).astype(jnp.bfloat16)
    value_low = (
        jnp.dot(flat_rows, value_proj, preferred_element_type=jnp.float32) + value_bias
    ).astype(jnp.bfloat16)
    key_here = key_low.reshape(row_count, local_len, features)
    value_here = value_low.reshape(row_count, local_len, features)
    key_all, value_all = (
        lax.all_gather(key_here, "seq", axis=1, tiled=True),
        lax.all_gather(value_here, "seq", axis=1, tiled=True),
    )
    key_units = to_units(key_all)
    value_units = to_units(value_all)
    context_units, log_units = lax.map(
        unit_forward, (query_units, key_units, value_units, query_segs, key_segs)
    )
    context = from_units(context_units).reshape(row_count * local_len, features)
    attended = jnp.dot(context, output_proj, preferred_element_type=jnp.float32) + output_bias
    first_resid = flat_wide + attended
    hidden = layer_norm(first_resid, first_gain, first_shift)
    hidden_low = hidden.astype(jnp.bfloat16)
    expanded = jnp.dot(hidden_low, expand_proj, preferred_element_type=jnp.float32) + expand_bias
    active = gelu_exact(expanded).astype(jnp.bfloat16)
    second_resid = (
        hidden + jnp.dot(active, shrink_proj, preferred_element_type=jnp.float32) + shrink_bias
    )
    outputs = layer_norm(second_resid, second_gain, second_shift)
    pooled_part = jnp.einsum(
        "rpt,rtd->rpd", members, outputs.reshape(row_count, local_len, features), precision=HIGH
    )
    pooled_sum = lax.psum(pooled_part, "seq")
    pooled = pooled_sum.reshape(own_count, features) / lengths_wide
    unit_vec, unit_pull = jax.vjp(normalize_rows, pooled)
    unit_low = unit_vec.astype(jnp.bfloat16)
    every_unit = lax.all_gather(unit_low, "dp", axis=0, tiled=True).astype(jnp.float32)
    own_unit = unit_low.astype(jnp.float32)
    own_ids = passage_start + jnp.arange(own_count, dtype=jnp.int32)
    own_partners = lax.dynamic_slice_in_dim(partners, passage_start, own_count, 0)
    passage_loss, weights_soft = contrast(own_unit, every_unit, own_ids, own_partners)
    local_grad = 100.0 * jnp.dot(weights_soft, every_unit, precision=HIGH)
    spread_terms = 100.0 * jnp.dot(weights_soft.T, own_unit, precision=HIGH)
    returned = lax.psum_scatter(spread_terms, "dp", scatter_dimension=0, tiled=True)
    grad_unit = local_grad + returned
    grad_pooled = (unit_pull(grad_unit)[0] / lengths_wide).reshape(row_count, pass_count, features)
    grad_out = jnp.einsum("rpt,rpd->rtd", members, grad_pooled, precision=HIGH).reshape(
        row_count * local_len, features
    )
    _, second_pull = jax.vjp(layer_norm, second_resid, second_gain, second_shift)
    grad_second, grad_second_gain, grad_second_shift = second_pull(grad_out)
    grad_shrunk = grad_second.astype(jnp.bfloat16)
    grad_shrink_proj = jnp.dot(active.T, grad_shrunk, preferred_element_type=jnp.float32)
    grad_shrink_bias = jnp.sum(grad_shrunk.astype(jnp.float32), 0)
    _, gelu_pull = jax.vjp(gelu_exact, expanded)
    grad_active = jnp.dot(grad_shrunk, shrink_proj.T, preferred_element_type=jnp.float32)
    grad_expanded = gelu_pull(grad_active)[0].astype(jnp.bfloat16)
    grad_expand_proj = jnp.dot(hidden_low.T, grad_expanded, preferred_element_type=jnp.float32)
    grad_expand_bias = jnp.sum(grad_expanded.astype(jnp.float32), 0)
    grad_hidden = grad_second + jnp.dot(
        grad_expanded, expand_proj.T, preferred_element_type=jnp.float32
    )
    _, first_pull = jax.vjp(layer_norm, first_resid, first_gain, first_shift)
    grad_first, grad_first_gain, grad_first_shift = first_pull(grad_hidden)
    grad_attended = grad_first.astype(jnp.bfloat16)
    grad_output_proj = jnp.dot(context.T, grad_attended, preferred_element_type=jnp.float32)
    grad_output_bias = jnp.sum(grad_attended.astype(jnp.float32), 0)
    grad_context = jnp.dot(grad_attended, output_proj.T, preferred_element_type=jnp.float32).astype(
        jnp.bfloat16
    )
    grad_context_units = to_units(grad_context.reshape(row_count, local_len, features))
    grad_query_units, grad_key_units, grad_value_units = lax.map(
        unit_back,
        (query_units, key_units, value_units, query_segs, key_segs, log_units, grad_context_units),
    )
    grad_query = from_units(grad_query_units).reshape(row_count * local_len, features)
    grad_key_all = from_units(grad_key_units)
    grad_value_all = from_units(grad_value_units)
    grad_keys, grad_values = (
        lax.psum_scatter(
            grad_key_all.astype(jnp.bfloat16), "seq", scatter_dimension=1, tiled=True
        ).astype(jnp.float32),
        lax.psum_scatter(
            grad_value_all.astype(jnp.bfloat16), "seq", scatter_dimension=1, tiled=True
        ).astype(jnp.float32),
    )
    grad_keys = grad_keys.astype(jnp.bfloat16).reshape(row_count * local_len, features)
    grad_values = grad_values.astype(jnp.bfloat16).reshape(row_count * local_len, features)
    grad_query_proj = jnp.dot(flat_rows.T, grad_query, preferred_element_type=jnp.float32)
    grad_query_bias = jnp.sum(grad_query.astype(jnp.float32), 0)
    grad_key_proj = jnp.dot(flat_rows.T, grad_keys, preferred_element_type=jnp.float32)
    grad_value_proj = jnp.dot(flat_rows.T, grad_values, preferred_element_type=jnp.float32)
    grad_value_bias = jnp.sum(grad_values.astype(jnp.float32), 0)
    tokens_grad = (
        grad_first
        + jnp.dot(grad_query, query_proj.T, preferred_element_type=jnp.float32)
        + jnp.dot(grad_keys, key_proj.T, preferred_element_type=jnp.float32)
        + jnp.dot(grad_values, value_proj.T, preferred_element_type=jnp.float32)
    )
    tokens_grad = tokens_grad.reshape(row_count, local_len, features)
    (
        grad_query_proj,
        grad_query_bias,
        grad_key_proj,
        grad_value_proj,
        grad_value_bias,
        grad_output_proj,
        grad_output_bias,
        grad_first_gain,
        grad_first_shift,
        grad_expand_proj,
        grad_expand_bias,
        grad_shrink_proj,
        grad_shrink_bias,
        grad_second_gain,
        grad_second_shift,
    ) = lax.psum(
        (
            grad_query_proj,
            grad_query_bias,
            grad_key_proj,
            grad_value_proj,
            grad_value_bias,
            grad_output_proj,
            grad_output_bias,
            grad_first_gain,
            grad_first_shift,
            grad_expand_proj,
            grad_expand_bias,
            grad_shrink_proj,
            grad_shrink_bias,
            grad_second_gain,
            grad_second_shift,
        ),
        ("dp", "seq"),
    )
    return (
        passage_loss,
        tokens_grad,
        grad_query_proj,
        grad_query_bias,
        grad_key_proj,
        grad_value_proj,
        grad_value_bias,
        grad_output_proj,
        grad_output_bias,
        grad_first_gain,
        grad_first_shift,
        grad_expand_proj,
        grad_expand_bias,
        grad_shrink_proj,
        grad_shrink_bias,
        grad_second_gain,
        grad_second_shift,
    )


def solution(mesh):
    placed = (
        P("dp", "seq", None),
        P("dp", None),
        P(),
        P(),
        P(),
        P(),
        P(),
        P(),
        P(),
        P(),
        P(),
        P(),
        P(),
        P(),
        P(),
        P(),
        P(),
        P(),
    )
    return jax.shard_map(
        body,
        mesh=mesh,
        in_specs=placed,
        out_specs=(
            P("dp"),
            P("dp", "seq", None),
            P(),
            P(),
            P(),
            P(),
            P(),
            P(),
            P(),
            P(),
            P(),
            P(),
            P(),
            P(),
            P(),
            P(),
            P(),
        ),
        check_vma=False,
    )
```

profile of v0, /device:TPU:0, one launch (start us, length us, event | category | flops | bytes accessed | tf_op | source)
XLA Modules:
  0.0 1419.9 jit_solution(8217197850460710516)
XLA Ops:
  55.4 229.4 %while.54 = (s32[]{:T(128)}, bf16[12,1024,64]{1,2,0:T(8,128)(2,1)}, f32[12,1024]{1,0:T(8,128)}, bf16[12,1024,64]{2,1,0:T(8,128)(2,1)}, s32[12,1024]{1,0:T(8,128)...) while((s32[]{:T(128)}, bf16[12,1024,64]{1,2,0:T(8,128)(2,1)}, ...), condition=%wide.region_7.8_spmd, body=%wide.region_2.7_spmd.sunk | while | flops 277904896 | bytes 32787312 | solution.py:183
  58.6 13.6 while.57
  77.7 13.6 while.57
  96.8 13.6 while.57
  115.9 13.6 while.57
  135.1 13.6 while.57
  154.2 13.6 while.57
  173.3 13.6 while.57
  192.4 13.6 while.57
  211.5 13.6 while.57
  230.6 13.6 while.57
  249.8 13.6 while.57
  268.9 13.6 while.57
  289.4 36.1 %multiply_convert_fusion.1 = (bf16[1024,3072]{1,0:T(8,128)(2,1)}, f32[1024,3072]{1,0:T(8,128)}, f32[1024,3072]{1,0:T(8,128)}) fusion(f32[3072]{0:T(1024)S(1)} %copy-done.53, bf16[768,3072]{1,0:T(8,128)(2,1)S(1)} %bitcast.260, f32[1024,768]{0,1:T(8,128)S(1)} %get-tuple-element.470, f32[768]{0:T(1024)S(1)} %copy-done.58, f32[768]{0:T(1024)S(1)} %copy-done.46, ...), kind=kOutput, calls=%fused_computation.59 | convolution fusion | flops 5043388416 | bytes 39348224 | tf_op jit(solution)/shard_map/dot_general | solution.py:191
  340.6 43.2 %all_gather.11 = bf16[256,768]{1,0:T(8,128)(2,1)S(1)} all-gather(bf16[16,768]{1,0:T(8,128)(2,1)S(1)} %multiply_convert_fusion.2), channel_id=1, replica_groups=mesh['dp'=16,'seq'=2] {'dp'}, dimensions={0}, use_global_device_ids=true | all-gather | bytes 417792 | tf_op jit(solution)/shard_map/all_gather | solution.py:204
  386.5 118.2 %reduce-scatter.4.cloned.1.call-done = f32[16,768]{1,0:T(8,128)} async-done(((f32[256,768]{1,0:T(8,128)}), f32[16,768]{1,0:T(8,128)}) %reduce-scatter.4.cloned.1.call-update) | async-done | bytes 49168 | tf_op jit(solution)/shard_map/reduce_scatter | solution.py:211
  528.8 17.8 %convert_reduce_fusion = (f32[3072]{0:T(1024)}, bf16[1024,3072]{1,0:T(8,128)(2,1)}) fusion(f32[1024,3072]{1,0:T(8,128)} %get-tuple-element.460, bf16[1024,768]{0,1:T(8,128)(2,1)S(1)} %get-tuple-element.450, bf16[3072,768]{1,0:T(8,128)(2,1)} %param.40, f32[1024,3072]{1,0:T(8,128)} %get-tuple-element.471, f32[3072]{0:T(1024)S(1)} %copy-done.53), kind=kOutput, calls=%fused_computation.57 | convolution fusion | flops 4885312512 | bytes 37773312 | tf_op jit(solution)/shard_map/dot_general | solution.py:223
  565.3 355.1 %while.56 = (s32[]{:T(128)}, bf16[12,1024,64]{1,2,0:T(8,128)(2,1)}, bf16[12,2048,64]{1,2,0:T(8,128)(2,1)}, bf16[12,2048,64]{1,2,0:T(8,128)(2,1)}, bf16[12,1024,6...) while((s32[]{:T(128)}, bf16[12,1024,64]{1,2,0:T(8,128)(2,1)}, ...), condition=%wide.region_27.28_spmd, body=%wide.region_23.27_spmd.sunk | while | flops 682294784 | bytes 76687968 | solution.py:239
  571.9 19.2 %while.58 = (s32[]{:T(128)}, f32[2048,64]{0,1:T(8,128)}, f32[2048,64]{0,1:T(8,128)S(1)}, bf16[2,512,64]{1,2,0:T(8,128)(2,1)}, s32[2,512]{1,0:T(2,128)S(1)}, /*in...) while((s32[]{:T(128)}, f32[2048,64]{0,1:T(8,128)}, ...), condition=%wide.region_26.26_spmd.clone, body=%wide.region_24.25_spmd.clone.sunk | while | flops 682294784 | bytes 72181064 | solution.py:155
  601.5 19.2 %while.58 = (s32[]{:T(128)}, f32[2048,64]{0,1:T(8,128)}, f32[2048,64]{0,1:T(8,128)S(1)}, bf16[2,512,64]{1,2,0:T(8,128)(2,1)}, s32[2,512]{1,0:T(2,128)S(1)}, /*in...) while((s32[]{:T(128)}, f32[2048,64]{0,1:T(8,128)}, ...), condition=%wide.region_26.26_spmd.clone, body=%wide.region_24.25_spmd.clone.sunk | while | flops 682294784 | bytes 72181064 | solution.py:155
  631.1 19.2 %while.58 = (s32[]{:T(128)}, f32[2048,64]{0,1:T(8,128)}, f32[2048,64]{0,1:T(8,128)S(1)}, bf16[2,512,64]{1,2,0:T(8,128)(2,1)}, s32[2,512]{1,0:T(2,128)S(1)}, /*in...) while((s32[]{:T(128)}, f32[2048,64]{0,1:T(8,128)}, ...), condition=%wide.region_26.26_spmd.clone, body=%wide.region_24.25_spmd.clone.sunk | while | flops 682294784 | bytes 72181064 | solution.py:155
  660.7 19.2 %while.58 = (s32[]{:T(128)}, f32[2048,64]{0,1:T(8,128)}, f32[2048,64]{0,1:T(8,128)S(1)}, bf16[2,512,64]{1,2,0:T(8,128)(2,1)}, s32[2,512]{1,0:T(2,128)S(1)}, /*in...) while((s32[]{:T(128)}, f32[2048,64]{0,1:T(8,128)}, ...), condition=%wide.region_26.26_spmd.clone, body=%wide.region_24.25_spmd.clone.sunk | while | flops 682294784 | bytes 72181064 | solution.py:155
  690.3 19.2 %while.58 = (s32[]{:T(128)}, f32[2048,64]{0,1:T(8,128)}, f32[2048,64]{0,1:T(8,128)S(1)}, bf16[2,512,64]{1,2,0:T(8,128)(2,1)}, s32[2,512]{1,0:T(2,128)S(1)}, /*in...) while((s32[]{:T(128)}, f32[2048,64]{0,1:T(8,128)}, ...), condition=%wide.region_26.26_spmd.clone, body=%wide.region_24.25_spmd.clone.sunk | while | flops 682294784 | bytes 72181064 | solution.py:155
  719.8 19.2 %while.58 = (s32[]{:T(128)}, f32[2048,64]{0,1:T(8,128)}, f32[2048,64]{0,1:T(8,128)S(1)}, bf16[2,512,64]{1,2,0:T(8,128)(2,1)}, s32[2,512]{1,0:T(2,128)S(1)}, /*in...) while((s32[]{:T(128)}, f32[2048,64]{0,1:T(8,128)}, ...), condition=%wide.region_26.26_spmd.clone, body=%wide.region_24.25_spmd.clone.sunk | while | flops 682294784 | bytes 72181064 | solution.py:155
  749.4 19.2 %while.58 = (s32[]{:T(128)}, f32[2048,64]{0,1:T(8,128)}, f32[2048,64]{0,1:T(8,128)S(1)}, bf16[2,512,64]{1,2,0:T(8,128)(2,1)}, s32[2,512]{1,0:T(2,128)S(1)}, /*in...) while((s32[]{:T(128)}, f32[2048,64]{0,1:T(8,128)}, ...), condition=%wide.region_26.26_spmd.clone, body=%wide.region_24.25_spmd.clone.sunk | while | flops 682294784 | bytes 72181064 | solution.py:155
  779.0 19.2 %while.58 = (s32[]{:T(128)}, f32[2048,64]{0,1:T(8,128)}, f32[2048,64]{0,1:T(8,128)S(1)}, bf16[2,512,64]{1,2,0:T(8,128)(2,1)}, s32[2,512]{1,0:T(2,128)S(1)}, /*in...) while((s32[]{:T(128)}, f32[2048,64]{0,1:T(8,128)}, ...), condition=%wide.region_26.26_spmd.clone, body=%wide.region_24.25_spmd.clone.sunk | while | flops 682294784 | bytes 72181064 | solution.py:155
  808.6 19.2 %while.58 = (s32[]{:T(128)}, f32[2048,64]{0,1:T(8,128)}, f32[2048,64]{0,1:T(8,128)S(1)}, bf16[2,512,64]{1,2,0:T(8,128)(2,1)}, s32[2,512]{1,0:T(2,128)S(1)}, /*in...) while((s32[]{:T(128)}, f32[2048,64]{0,1:T(8,128)}, ...), condition=%wide.region_26.26_spmd.clone, body=%wide.region_24.25_spmd.clone.sunk | while | flops 682294784 | bytes 72181064 | solution.py:155
  838.2 19.2 %while.58 = (s32[]{:T(128)}, f32[2048,64]{0,1:T(8,128)}, f32[2048,64]{0,1:T(8,128)S(1)}, bf16[2,512,64]{1,2,0:T(8,128)(2,1)}, s32[2,512]{1,0:T(2,128)S(1)}, /*in...) while((s32[]{:T(128)}, f32[2048,64]{0,1:T(8,128)}, ...), condition=%wide.region_26.26_spmd.clone, body=%wide.region_24.25_spmd.clone.sunk | while | flops 682294784 | bytes 72181064 | solution.py:155
  867.8 19.2 %while.58 = (s32[]{:T(128)}, f32[2048,64]{0,1:T(8,128)}, f32[2048,64]{0,1:T(8,128)S(1)}, bf16[2,512,64]{1,2,0:T(8,128)(2,1)}, s32[2,512]{1,0:T(2,128)S(1)}, /*in...) while((s32[]{:T(128)}, f32[2048,64]{0,1:T(8,128)}, ...), condition=%wide.region_26.26_spmd.clone, body=%wide.region_24.25_spmd.clone.sunk | while | flops 682294784 | bytes 72181064 | solution.py:155
  897.4 19.2 %while.58 = (s32[]{:T(128)}, f32[2048,64]{0,1:T(8,128)}, f32[2048,64]{0,1:T(8,128)S(1)}, bf16[2,512,64]{1,2,0:T(8,128)(2,1)}, s32[2,512]{1,0:T(2,128)S(1)}, /*in...) while((s32[]{:T(128)}, f32[2048,64]{0,1:T(8,128)}, ...), condition=%wide.region_26.26_spmd.clone, body=%wide.region_24.25_spmd.clone.sunk | while | flops 682294784 | bytes 72181064 | solution.py:155
  968.0 42.7 %all-reduce = (f32[768]{0:T(1024)}, f32[768]{0:T(1024)}, f32[768]{0:T(1024)}, f32[768]{0:T(1024)}, f32[768]{0:T(1024)}, /*index=5*/f32[3072]{0:T(1024)}, f32[768]{0:T(1024)}, f32[768]{0:T(1024)}, f32[768]{0:T(1024)}) all-reduce(f32[768]{0:T(1024)S(1)} %reduce_sum.239, ...), channel_id=1, replica_groups=mesh['dp'=16,'seq'=2] {'dp','seq'}, use_global_device_ids=true, to_apply=%region_32.33 | all-reduce | flops 9216 | bytes 73728 | tf_op jit(solution)/shard_map/psum | solution.py:284
  1010.7 379.0 %all-reduce.4.cloned.1.call-done = (f32[768,768]{0,1:T(8,128)}, f32[768,768]{0,1:T(8,128)}, f32[768,768]{0,1:T(8,128)}, f32[768,768]{1,0:T(8,128)}, f32[768,3072]{1,0:T(8,128)}, /*index=5*/f32[3072,768]{1,0:T(8,128)}) async-done(((f32[768,768]{0,1:T(8,128)}, f32[768,768]{0,1:T(8,128)}, f32[768,768]{0,1:T(8,128)}, f32[768,768]{1,0:T(8,128)}, f32[768,3072]{1,0:T(8,128)}, /*index=5*/f32[3072,768]{1,0:T(8,128)}), ...) | async-done | bytes 28311568 | tf_op jit(solution)/shard_map/psum | solution.py:284
  (1233 shorter events, 762.3 us)
Async XLA Ops:
  7.2 277.6 %copy-start = (bf16[768,768]{1,0:T(8,128)(2,1)S(1)}, bf16[768,768]{1,0:T(8,128)(2,1)}, u32[]{:S(2)}) copy-start(bf16[768,768]{1,0:T(8,128)(2,1)} %param.34) | copy-start | bytes 3538948
  7.2 4.6 copy-start.22
  7.2 4.6 copy-start.54
  7.2 20.2 %all-gather.5.cloned.1.call-start = ((), (), s32[]{:S(2)}) async-start(), calls=%async_computation.6 | async-start | bytes 4718592 | tf_op jit(solution)/shard_map/all_gather | solution.py:178
  11.7 30.4 %all-gather.7.cloned.1.call-start = ((), (), s32[]{:S(2)}) async-start(), calls=%async_computation.7 | async-start | bytes 4718592 | tf_op jit(solution)/shard_map/all_gather | solution.py:179
  15.6 489.1 %reduce-scatter.4.cloned.1.call-start = ((), (), s32[]{:S(2)}) async-start(), calls=%async_computation.3 | async-start | bytes 835584 | tf_op jit(solution)/shard_map/reduce_scatter | solution.py:211
  25.8 27.7 %copy-start.29 = (s32[1024]{0:T(1024)}, s32[1024]{0:T(1024)S(1)}, u32[]{:S(2)}) copy-start(s32[1024]{0:T(1024)S(1)} %dynamic-slice.3) | copy-start | bytes 12292
  55.4 229.4 %copy-start.56 = (f32[768]{0:T(1024)S(1)}, f32[768]{0:T(1024)}, u32[]{:S(2)}) copy-start(f32[768]{0:T(1024)} %param.35) | copy-start | bytes 9220
  284.8 40.6 %slice-start.3 = ((s8[4718592]{0:T(1024)(128)(4,1)}), s8[4194304]{0:T(1024)(128)(4,1)S(1)}, s32[]{:S(2)}) async-start(s8[4718592]{0:T(1024)(128)(4,1)} %bitcast.257), calls=%async_computation.12 | async-start | bytes 8388608
  288.6 36.9 %copy-start.14 = (f32[1024,768]{0,1:T(8,128)}, f32[1024,768]{0,1:T(8,128)S(1)}, u32[]{:S(2)}) copy-start(f32[1024,768]{0,1:T(8,128)S(1)} %get-tuple-element.470) | copy-start | bytes 9437188
  288.6 268.8 %copy-start.31 = (f32[1024]{0:T(1024)}, f32[1024]{0:T(1024)S(1)}, u32[]{:S(2)}) copy-start(f32[1024]{0:T(1024)S(1)} %broadcast_multiply_fusion.1) | copy-start | bytes 12292
  289.4 268.1 %copy-start.36 = (f32[1024]{0:T(1024)}, f32[1024]{0:T(1024)S(1)}, u32[]{:S(2)}) copy-start(f32[1024]{0:T(1024)S(1)} %fusion.69) | copy-start | bytes 12292
  289.4 36.1 %slice-start.4 = ((s8[4718592]{0:T(1024)(128)(4,1)}), s8[524288]{0:T(1024)(128)(4,1)S(1)}, s32[]{:S(2)}) async-start(s8[4718592]{0:T(1024)(128)(4,1)} %bitcast.257), calls=%async_computation.13 | async-start | bytes 1048576
  289.4 36.1 %copy-start.57 = (f32[768]{0:T(1024)S(1)}, f32[768]{0:T(1024)}, u32[]{:S(2)}) copy-start(f32[768]{0:T(1024)} %param.41) | copy-start | bytes 9220
  333.2 7.1 copy-start.43
  333.2 50.7 %copy-start.50 = (s32[16]{0:T(128)S(1)}, s32[16]{0:T(128)}, u32[]{:S(2)}) copy-start(s32[16]{0:T(128)} %iota_add_fusion) | copy-start | bytes 196
  333.2 51.0 %copy-start.44 = (s32[16]{0:T(128)S(1)}, s32[16]{0:T(128)}, u32[]{:S(2)}) copy-start(s32[16]{0:T(128)} %dynamic_slice.66) | copy-start | bytes 196
  386.5 558.3 %reduce-scatter.8.cloned.1.call-start = ((), (), s32[]{:S(2)}) async-start(), calls=%async_computation.5 | async-start | bytes 4718592 | tf_op jit(solution)/shard_map/reduce_scatter | solution.py:250
  521.7 4.7 copy-start.13
  528.4 18.2 %copy-start.24 = (bf16[1024,768]{0,1:T(8,128)(2,1)}, bf16[1024,768]{0,1:T(8,128)(2,1)S(1)}, u32[]{:S(2)}) copy-start(bf16[1024,768]{0,1:T(8,128)(2,1)S(1)} %get-tuple-element.450) | copy-start | bytes 4718596
  528.8 17.8 %copy-start.15 = (f32[1024,768]{0,1:T(8,128)S(1)}, f32[1024,768]{0,1:T(8,128)}, u32[]{:S(2)}) copy-start(f32[1024,768]{0,1:T(8,128)} %copy-done.14) | copy-start | bytes 9437188
  920.4 29.0 %reduce-scatter.6.cloned.1.call-start = ((), (), s32[]{:S(2)}) async-start(), calls=%async_computation.4 | async-start | bytes 4718592 | tf_op jit(solution)/shard_map/reduce_scatter | solution.py:247
  921.0 5.0 copy-start.19
  921.0 468.7 %all-reduce.4.cloned.1.call-start = ((), (), s32[]{:S(2)}) async-start(), calls=%async_computation.8 | async-start | bytes 56623104 | tf_op jit(solution)/shard_map/psum | solution.py:284
  921.1 4.9 copy-start.23
  921.1 7.8 copy-start.62
  926.1 11.0 slice-start.7
  928.9 8.1 copy-start.25
  928.9 8.1 slice-start.8
  1398.0 10.7 slice-start
  1399.5 9.3 slice-start.1
  1399.5 9.3 slice-start.2
  (207 other events, 471.0 us)
Sparse Core Ops, SparseCore 0:
  11.8 14.8 all-gather.4
  28.8 13.2 all-gather.6
  386.6 118.0 reduce-scatter.3
  920.5 9.9 reduce-scatter.7
  932.8 12.0 reduce-scatter.5
  954.2 435.4 all-reduce.3
where the time goes:
time: 1440 us; the launch traced here: 1420 us
  waiting for transfers between devices  501 us (35%)
  matrix products  405 us (28%)
  local copies, waits for them, and re-layouts  364 us (25%)
  blocking collectives  89.5 us (6%)
  other arithmetic  39.4 us (3%)
  between operations  15.4 us (1%)
    psum x1, waiting for transfers between devices, body(): lax.psum((grad_query_proj, grad_query_bias, grad_key_proj, grad_value_pro...  379 us
    reduce_scatter x1, waiting for transfers between devices, body(): lax.psum_scatter(spread_terms, 'dp', scatter_dimension=0, tiled=True)  118 us
    while x348, local copies, waits for them, and re-layouts  94.4 us
    dot_general x24, matrix products, one_block(): jnp.dot(probs, value_unit, preferred_element_type=jnp.float32)  75.7 us
    dynamic_slice x84, local copies, waits for them, and re-layouts, body(): lax.map(unit_forward, (query_units, key_units, value_units, query_segs, k...  65.1 us
    dot_general x48, matrix products, score_block(): jnp.einsum('qe,ke->qk', query_block, key_unit, preferred_element_type=jnp...  57.3 us
    dot_general x24, matrix products, step(): jnp.einsum('qk,qe->ke', grad_scores, query_block, preferred_element_type=...  46.3 us
    all_gather x1, blocking collectives, body(): lax.all_gather(unit_low, 'dp', axis=0, tiled=True).astype(jnp.float32)  43.2 us
  transfers between devices with their start and end apart: 6, of which 3 were waited for; matrix products, arithmetic and copies ran while one was open for 5% of the time, Pallas kernels for 0%

commit v1 on v0

v1 whole, which is shorter than its diff:
```python
import functools
import math

import jax
import jax.numpy as jnp
from jax import lax
from jax.experimental import pallas as pl
from jax.experimental.pallas import tpu as pltpu
from jax.sharding import PartitionSpec as P

HEADS = 12
EPS_NORM = 1e-12
BIG_NEG = -1000000000.0
HIGH = lax.Precision.HIGHEST
BF = jnp.bfloat16
F32 = jnp.float32
TILE = 128
MASKED = -float(2**30)
VMEM_MIB = 1 << 20


def dot(left, right, over=((1,), (0,))):
    return lax.dot_general(left, right, (over, ((), ())), preferred_element_type=F32)


def split3(value):
    high = value.astype(BF)
    rest = value - high.astype(F32)
    middle = rest.astype(BF)
    low = (rest - middle.astype(F32)).astype(BF)
    return high, middle, low


def lane_masks():
    lane = lax.broadcasted_iota(jnp.int32, (1, 2 * TILE), 1) % TILE
    even = jnp.where(lane < TILE // 2, 1.0, 0.0).astype(BF)
    odd = jnp.where(lane < TILE // 2, 0.0, 1.0).astype(BF)
    return even, odd


def stack_heads(pair, even, odd):
    return jnp.concatenate([pair * even, pair * odd], 0)


def row_scalar_lanes(value):
    lane = lax.broadcasted_iota(jnp.int32, (1, TILE), 1) % (TILE // 2)
    high = value.astype(BF).astype(F32)
    rest = value - high
    middle = rest.astype(BF).astype(F32)
    low = rest - middle
    return jnp.where(
        lane == 32, high, jnp.where(lane == 33, middle, jnp.where(lane == 34, low, 0.0))
    ).astype(BF)


def attend_kernel(
    lo_ref, hi_ref, q_ref, one_ref, k_ref, v_ref, aux_ref, c_ref, cb_ref, qaux_ref, s_scr, m_scr, o_scr
):
    lo, hi = lo_ref[pl.program_id(0)], hi_ref[pl.program_id(0)]
    pairs = q_ref.shape[1] // TILE
    even, odd = lane_masks()
    m_scr[...] = jnp.full(m_scr.shape, 2.0 * MASKED, F32)
    o_scr[...] = jnp.zeros(o_scr.shape, F32)
    ones_even = jnp.broadcast_to(even[:, :TILE], (TILE, TILE))
    ones_odd = jnp.broadcast_to(odd[:, :TILE], (TILE, TILE))

    def scores(t, carry):
        rows = pl.ds(pl.multiple_of(t * TILE, TILE), TILE)
        aux = aux_ref[rows, :]
        for j in range(pairs):
            cols = slice(j * TILE, (j + 1) * TILE)
            keys = stack_heads(jnp.concatenate([k_ref[rows, cols], aux], 1), even, odd)
            queries = jnp.concatenate([q_ref[:, cols], one_ref[...]], 1)
            s = dot(queries, keys, ((1,), (1,)))
            s_scr[t - lo, j] = s
            m_scr[j] = jnp.maximum(m_scr[j], s)
        return carry

    lax.fori_loop(lo, hi, scores, 0)
    for j in range(pairs):
        m = m_scr[j]
        top_even = jnp.max(m[:, :TILE], 1, keepdims=True)
        top_odd = jnp.max(m[:, TILE:], 1, keepdims=True)
        m_scr[j] = jnp.concatenate(
            [jnp.broadcast_to(top_even, (TILE, TILE)), jnp.broadcast_to(top_odd, (TILE, TILE))], 1
        )

    def weigh(t, carry):
        rows = pl.ds(pl.multiple_of(t * TILE, TILE), TILE)
        for j in range(pairs):
            cols = slice(j * TILE, (j + 1) * TILE)
            p = jnp.exp(s_scr[t - lo, j] - m_scr[j]).astype(BF)
            v = v_ref[rows, cols]
            values = jnp.concatenate(
                [
                    jnp.concatenate([v * even[:, :TILE], ones_even], 1),
                    jnp.concatenate([v * odd[:, :TILE], ones_odd], 1),
                ],
                0,
            )
            o_scr[j] += dot(p, values)
        return carry

    lax.fori_loop(lo, hi, weigh, 0)
    first = lax.broadcasted_iota(jnp.int32, (1, TILE), 1) < TILE // 2
    for j in range(pairs):
        cols = slice(j * TILE, (j + 1) * TILE)
        total = o_scr[j][:, TILE:]
        c = o_scr[j][:, :TILE] / total
        c_ref[:, cols] = c
        cb_ref[:, cols] = c.astype(BF)
        top = jnp.where(first, m_scr[j][:, :TILE], m_scr[j][:, TILE:])
        qaux_ref[:, cols] = row_scalar_lanes(top + jnp.log(total)) + one_ref[...]


def attend(queries, one_hot, keys, values, aux, lo, hi):
    length, features = queries.shape
    window = keys.shape[0]
    pairs = features // TILE
    row = lambda i, *_: (i, 0)
    whole = lambda i, *_: (0, 0)
    return pl.pallas_call(
        attend_kernel,
        grid_spec=pltpu.PrefetchScalarGridSpec(
            num_scalar_prefetch=2,
            grid=(length // TILE,),
            in_specs=[
                pl.BlockSpec((TILE, features), row),
                pl.BlockSpec((TILE, TILE), row),
                pl.BlockSpec((window, features), whole),
                pl.BlockSpec((window, features), whole),
                pl.BlockSpec((window, TILE), whole),
            ],
            out_specs=[pl.BlockSpec((TILE, features), row)] * 3,
            scratch_shapes=[
                pltpu.VMEM((window // TILE, pairs, TILE, 2 * TILE), F32),
                pltpu.VMEM((pairs, TILE, 2 * TILE), F32),
                pltpu.VMEM((pairs, TILE, 2 * TILE), F32),
            ],
        ),
        out_shape=[
            jax.ShapeDtypeStruct((length, features), F32),
            jax.ShapeDtypeStruct((length, features), BF),
            jax.ShapeDtypeStruct((length, features), BF),
        ],
        compiler_params=pltpu.CompilerParams(vmem_limit_bytes=40 * VMEM_MIB),
        name="attend",
    )(lo, hi, queries, one_hot, keys, values, aux)


def attend_back_kernel(
    lo_ref, hi_ref, q_ref, qaux_ref, dc_ref, c_ref, k_ref, v_ref, aux_ref,
    dq_ref, dk_ref, dv_ref, dqt_scr, daux_scr, dk_scr, dv_scr,
):
    step = pl.program_id(0)
    pairs = q_ref.shape[1] // TILE
    tiles = q_ref.shape[0] // TILE
    even, odd = lane_masks()

    @pl.when(step == 0)
    def _():
        dqt_scr[...] = jnp.zeros(dqt_scr.shape, F32)
        lane = lax.broadcasted_iota(jnp.int32, (TILE, TILE), 0) // (TILE // 2)
        other = lax.broadcasted_iota(jnp.int32, (TILE, TILE), 1) // (TILE // 2)
        same_head = jnp.where(lane == other, 1.0, 0.0).astype(BF)

        def deltas(i, carry):
            rows = pl.ds(pl.multiple_of(i * TILE, TILE), TILE)
            for j in range(pairs):
                cols = slice(j * TILE, (j + 1) * TILE)
                product = dc_ref[rows, cols].astype(F32) * c_ref[rows, cols]
                high, middle, low = split3(product)
                delta = dot(high, same_head) + dot(middle, same_head) + dot(low, same_head)
                daux_scr[rows, cols] = row_scalar_lanes(delta)
            return carry

        lax.fori_loop(0, tiles, deltas, 0)

    dk_scr[...] = jnp.zeros(dk_scr.shape, F32)
    dv_scr[...] = jnp.zeros(dv_scr.shape, F32)

    def tile(i, carry):
        rows = pl.ds(pl.multiple_of(i * TILE, TILE), TILE)
        for j in range(pairs):
            cols = slice(j * TILE, (j + 1) * TILE)
            k = k_ref[:, cols]
            keys = jnp.concatenate([k, aux_ref[...]], 1)
            values = jnp.concatenate([v_ref[:, cols], aux_ref[...]], 1)
            queries = stack_heads(jnp.concatenate([q_ref[rows, cols], qaux_ref[rows, cols]], 1), even, odd)
            grads = stack_heads(jnp.concatenate([dc_ref[rows, cols], daux_scr[rows, cols]], 1), even, odd)
            p = jnp.exp(dot(keys, queries, ((1,), (1,))))
            ds = (p * dot(values, grads, ((1,), (1,)))).astype(BF)
            dv_scr[j] += dot(p.astype(BF), grads[:, :TILE])
            dk_scr[j] += dot(ds, queries[:, :TILE])
            keys_t = jnp.concatenate([(k * even[:, :TILE]).T, (k * odd[:, :TILE]).T], 1)
            dqt_scr[j, :, rows] += dot(keys_t, jnp.concatenate([ds[:, :TILE], ds[:, TILE:]], 0))
        return carry

    lax.fori_loop(lo_ref[step], hi_ref[step], tile, 0)
    for j in range(pairs):
        cols = slice(j * TILE, (j + 1) * TILE)
        dk_ref[:, cols] = dk_scr[j].astype(BF)
        dv_ref[:, cols] = dv_scr[j].astype(BF)

    @pl.when(step == pl.num_programs(0) - 1)
    def _():
        for i in range(tiles):
            for j in range(pairs):
                block = dqt_scr[j, :, i * TILE : (i + 1) * TILE] * 0.125
                dq_ref[i * TILE : (i + 1) * TILE, j * TILE : (j + 1) * TILE] = block.T.astype(BF)


def attend_back(queries, qaux, grad_context, context, keys, values, aux, lo, hi):
    length, features = queries.shape
    window = keys.shape[0]
    pairs = features // TILE
    row = lambda i, *_: (i, 0)
    whole = lambda i, *_: (0, 0)
    return pl.pallas_call(
        attend_back_kernel,
        grid_spec=pltpu.PrefetchScalarGridSpec(
            num_scalar_prefetch=2,
            grid=(window // TILE,),
            in_specs=[pl.BlockSpec((length, features), whole)] * 4
            + [
                pl.BlockSpec((TILE, features), row),
                pl.BlockSpec((TILE, features), row),
                pl.BlockSpec((TILE, TILE), row),
            ],
            out_specs=[
                pl.BlockSpec((length, features), whole),
                pl.BlockSpec((TILE, features), row),
                pl.BlockSpec((TILE, features), row),
            ],
            scratch_shapes=[
                pltpu.VMEM((pairs, TILE, length), F32),
                pltpu.VMEM((length, features), BF),
                pltpu.VMEM((pairs, TILE, TILE), F32),
                pltpu.VMEM((pairs, TILE, TILE), F32),
            ],
        ),
        out_shape=[
            jax.ShapeDtypeStruct((length, features), BF),
            jax.ShapeDtypeStruct((window, features), BF),
            jax.ShapeDtypeStruct((window, features), BF),
        ],
        compiler_params=pltpu.CompilerParams(vmem_limit_bytes=40 * VMEM_MIB),
        name="attend_back",
    )(lo, hi, queries, qaux, grad_context, context, keys, values, aux)


def gelu_parts(u):
    size = jnp.abs(u)
    base = 1.0 + (0.3275911 * math.sqrt(0.5)) * size
    t = pl.reciprocal(base, approx=True)
    t = t * (2.0 - base * t)
    bell = jnp.exp(-0.5 * (u * u))
    poly = t * (0.127414796 + t * (-0.142248368 + t * (0.7107068705 + t * (-0.7265760135 + t * 0.5307027145))))
    tail = poly * bell
    below = jnp.where(u < 0.0, tail, 1.0 - tail)
    return u * below, below + u * bell * (1.0 / math.sqrt(2.0 * math.pi))


def normalized(resid):
    center = resid - jnp.mean(resid, -1, keepdims=True)
    scale = lax.rsqrt(jnp.mean(center * center, -1, keepdims=True) + EPS_NORM)
    return center * scale, scale


def feed_kernel(
    cb_ref, x_ref, member_ref, wo_ref, bo_ref, g1_ref, b1_ref, w1_ref, be_ref, w2_ref, bs_ref, g2_ref, b2_ref,
    n1_ref, r1_ref, h_ref, f_ref, gp_ref, n2_ref, r2_ref, pool_ref,
):
    attended = dot(cb_ref[...], wo_ref[...]) + bo_ref[...]
    unit, scale = normalized(x_ref[...].astype(F32) + attended)
    n1_ref[...] = unit.astype(BF)
    r1_ref[...] = scale
    hidden = unit * g1_ref[...] + b1_ref[...]
    low = hidden.astype(BF)
    h_ref[...] = low
    resid = hidden + bs_ref[...]
    chunk = 512
    for start in range(0, w1_ref.shape[1], chunk):
        cols = slice(start, start + chunk)
        u = dot(low, w1_ref[:, cols]) + be_ref[:, cols]
        active, slope = gelu_parts(u)
        active = active.astype(BF)
        f_ref[:, cols] = active
        gp_ref[:, cols] = slope.astype(BF)
        resid = resid + dot(active, w2_ref[cols, :])
    unit, scale = normalized(resid)
    n2_ref[...] = unit.astype(BF)
    r2_ref[...] = scale
    out = unit * g2_ref[...] + b2_ref[...]
    high, middle, _ = split3(out)
    part = dot(member_ref[...], high) + dot(member_ref[...], middle)

    @pl.when(pl.program_id(0) == 0)
    def _():
        pool_ref[...] = part

    @pl.when(pl.program_id(0) > 0)
    def _():
        pool_ref[...] += part


def feed(cb, x, member, wo, bo, g1, b1, w1, be, w2, bs, g2, b2):
    length, features = x.shape
    hidden = w1.shape[1]
    pass_count = member.shape[0]
    rows = 256
    row = lambda i: (i, 0)
    whole = lambda i: (0, 0)
    once = pl.Buffered(1)

    def full(array):
        return pl.BlockSpec(array.shape, whole, pipeline_mode=once)

    return pl.pallas_call(
        feed_kernel,
        grid=(length // rows,),
        in_specs=[
            pl.BlockSpec((rows, features), row),
            pl.BlockSpec((rows, features), row),
            pl.BlockSpec((pass_count, rows), lambda i: (0, i)),
        ]
        + [full(a) for a in (wo, bo, g1, b1, w1, be, w2, bs, g2, b2)],
        out_specs=[
            pl.BlockSpec((rows, features), row),
            pl.BlockSpec((rows, 1), row),
            pl.BlockSpec((rows, features), row),
            pl.BlockSpec((rows, hidden), row),
            pl.BlockSpec((rows, hidden), row),
            pl.BlockSpec((rows, features), row),
            pl.BlockSpec((rows, 1), row),
            pl.BlockSpec((pass_count, features), whole),
        ],
        out_shape=[
            jax.ShapeDtypeStruct((length, features), BF),
            jax.ShapeDtypeStruct((length, 1), F32),
            jax.ShapeDtypeStruct((length, features), BF),
            jax.ShapeDtypeStruct((length, hidden), BF),
            jax.ShapeDtypeStruct((length, hidden), BF),
            jax.ShapeDtypeStruct((length, features), BF),
            jax.ShapeDtypeStruct((length, 1), F32),
            jax.ShapeDtypeStruct((pass_count, features), F32),
        ],
        compiler_params=pltpu.CompilerParams(vmem_limit_bytes=48 * VMEM_MIB),
        name="feed",
    )(cb, x, member, wo, bo, g1, b1, w1, be, w2, bs, g2, b2)


def norm_back(grad, unit, scale, gain):
    wide = grad * gain
    return scale * (
        wide - jnp.mean(wide, -1, keepdims=True) - unit * jnp.mean(wide * unit, -1, keepdims=True)
    )


def add_rows(ref, row, value):
    ref[row : row + 1, :] += jnp.sum(value, 0, keepdims=True)


def start_back_kernel(spread_ref, pooled_ref, n2_ref, r2_ref, g2_ref, dr_ref, dy_ref, sums_ref):
    @pl.when(pl.program_id(0) == 0)
    def _():
        sums_ref[...] = jnp.zeros(sums_ref.shape, F32)

    grad = dot(spread_ref[...], pooled_ref[...])
    unit = n2_ref[...].astype(F32)
    add_rows(sums_ref, 0, grad * unit)
    add_rows(sums_ref, 1, grad)
    dr = norm_back(grad, unit, r2_ref[...], g2_ref[...])
    dr_ref[...] = dr
    dy = dr.astype(BF)
    dy_ref[...] = dy
    add_rows(sums_ref, 2, dy.astype(F32))


def start_back(spread, pooled_parts, n2, r2, g2):
    length, features = n2.shape
    rows = 256
    row = lambda i: (i, 0)
    whole = lambda i: (0, 0)
    return pl.pallas_call(
        start_back_kernel,
        grid=(length // rows,),
        in_specs=[
            pl.BlockSpec((rows, spread.shape[1]), row),
            pl.BlockSpec(pooled_parts.shape, whole),
            pl.BlockSpec((rows, features), row),
            pl.BlockSpec((rows, 1), row),
            pl.BlockSpec((1, features), whole),
        ],
        out_specs=[
            pl.BlockSpec((rows, features), row),
            pl.BlockSpec((rows, features), row),
            pl.BlockSpec((8, features), whole),
        ],
        out_shape=[
            jax.ShapeDtypeStruct((length, features), F32),
            jax.ShapeDtypeStruct((length, features), BF),
            jax.ShapeDtypeStruct((8, features), F32),
        ],
        name="start_back",
    )(spread, pooled_parts, n2, r2, g2)


def feed_back_kernel(
    dr2_ref, dy_ref, gp_ref, n1_ref, r1_ref, w2_ref, w1_ref, wo_ref, g1_ref,
    du_ref, dr1_ref, da_ref, dc_ref, sums_ref, wide_sums_ref,
):
    @pl.when(pl.program_id(0) == 0)
    def _():
        sums_ref[...] = jnp.zeros(sums_ref.shape, F32)
        wide_sums_ref[...] = jnp.zeros(wide_sums_ref.shape, F32)

    dy = dy_ref[...]
    dh = dr2_ref[...]
    chunk = 512
    for start in range(0, w1_ref.shape[1], chunk):
        cols = slice(start, start + chunk)
        slope = gp_ref[:, cols].astype(F32)
        du = (slope * dot(dy, w2_ref[cols, :], ((1,), (1,)))).astype(BF)
        du_ref[:, cols] = du
        wide_sums_ref[0:1, cols] += jnp.sum(du.astype(F32), 0, keepdims=True)
        dh = dh + dot(du, w1_ref[:, cols], ((1,), (1,)))
    unit = n1_ref[...].astype(F32)
    add_rows(sums_ref, 0, dh * unit)
    add_rows(sums_ref, 1, dh)
    dr = norm_back(dh, unit, r1_ref[...], g1_ref[...])
    dr1_ref[...] = dr
    da = dr.astype(BF)
    da_ref[...] = da
    add_rows(sums_ref, 2, da.astype(F32))
    dc_ref[...] = dot(da, wo_ref[...], ((1,), (1,))).astype(BF)


def feed_back(dr2, dy, gp, n1, r1, w2, w1, wo, g1):
    length, features = dy.shape
    hidden = gp.shape[1]
    rows = 256
    row = lambda i: (i, 0)
    whole = lambda i: (0, 0)
    once = pl.Buffered(1)

    def full(array):
        return pl.BlockSpec(array.shape, whole, pipeline_mode=once)

    return pl.pallas_call(
        feed_back_kernel,
        grid=(length // rows,),
        in_specs=[
            pl.BlockSpec((rows, features), row),
            pl.BlockSpec((rows, features), row),
            pl.BlockSpec((rows, hidden), row),
            pl.BlockSpec((rows, features), row),
            pl.BlockSpec((rows, 1), row),
            full(w2),
            full(w1),
            full(wo),
            full(g1),
        ],
        out_specs=[
            pl.BlockSpec((rows, hidden), row),
            pl.BlockSpec((rows, features), row),
            pl.BlockSpec((rows, features), row),
            pl.BlockSpec((rows, features), row),
            pl.BlockSpec((8, features), whole),
            pl.BlockSpec((8, hidden), whole),
        ],
        out_shape=[
            jax.ShapeDtypeStruct((length, hidden), BF),
            jax.ShapeDtypeStruct((length, features), F32),
            jax.ShapeDtypeStruct((length, features), BF),
            jax.ShapeDtypeStruct((length, features), BF),
            jax.ShapeDtypeStruct((8, features), F32),
            jax.ShapeDtypeStruct((8, hidden), F32),
        ],
        compiler_params=pltpu.CompilerParams(vmem_limit_bytes=48 * VMEM_MIB),
        name="feed_back",
    )(dr2, dy, gp, n1, r1, w2, w1, wo, g1)


def swap_seq(array):
    return lax.ppermute(array, "seq", [(0, 1), (1, 0)])


def swap_dp(array, bit):
    count = lax.axis_size("dp")
    return lax.ppermute(array, "dp", [(i, i ^ (1 << bit)) for i in range(count)])


def pick_half(array, axis, which):
    half = array.shape[axis] // 2
    return lax.dynamic_slice_in_dim(array, which * half, half, axis)


def join(mine, other, axis, place):
    return jnp.where(
        place == 0, jnp.concatenate([mine, other], axis), jnp.concatenate([other, mine], axis)
    )


def halving_axis(shape):
    rows, cols = shape
    if rows % 32 == 0:
        return 0
    if cols % 256 == 0:
        return 1
    return 0


def reduce_block(block, order):
    index = lax.axis_index("dp")
    axes = []
    for bit in order:
        place = (index >> bit) & 1
        axis = halving_axis(block.shape)
        axes.append(axis)
        other = swap_dp(pick_half(block, axis, 1 - place), bit)
        block = (pick_half(block, axis, place).astype(F32) + other.astype(F32)).astype(BF)
    for bit, axis in zip(reversed(order), reversed(axes)):
        place = (index >> bit) & 1
        block = join(block, swap_dp(block, bit), axis, place)
    return block


def reduce_all(partial, groups, axis, turn):
    seq = lax.axis_index("seq")
    bits = int(math.log2(lax.axis_size("dp")))
    orders = [list(range(bits)), [1, 0] + list(range(2, bits)), list(range(2, bits)) + [0, 1]]
    other = swap_seq(pick_half(partial, 0, 1 - seq))
    half = (pick_half(partial, 0, seq).astype(F32) + other.astype(F32)).astype(BF)
    pieces = jnp.split(half, groups, axis) if groups > 1 else [half]
    done = [reduce_block(piece, orders[(turn + i) % 3]) for i, piece in enumerate(pieces)]
    half = jnp.concatenate(done, axis) if groups > 1 else done[0]
    return join(half, swap_seq(half), 0, seq).astype(F32)


def sum_small(array):
    array = array + swap_seq(array)
    for bit in range(int(math.log2(lax.axis_size("dp")))):
        array = array + swap_dp(array, bit)
    return array


def body(
    tokens, lengths, partners, query_proj, query_bias, key_proj, value_proj, value_bias, output_proj, output_bias,
    first_gain, first_shift, expand_proj, expand_bias, shrink_proj, shrink_bias, second_gain, second_shift,
):
    _, length, features = tokens.shape
    pass_count = lengths.shape[1]
    seq = lax.axis_index("seq")
    dp = lax.axis_index("dp")
    far = length // 2
    window = length + far
    x = tokens[0]

    x_far = swap_seq(lax.dynamic_slice_in_dim(x, (1 - seq) * far, far, 0))
    x_window = join(x, x_far, 0, seq)

    ends = jnp.cumsum(lengths[0])
    bounds = jnp.concatenate([jnp.zeros(1, jnp.int32), ends, jnp.full(1, 2 * length, jnp.int32)])
    window_start = seq * far
    own_start = seq * length
    positions = window_start + jnp.arange(window, dtype=jnp.int32)
    segment = jnp.sum((positions[:, None] >= ends[None, :]).astype(jnp.int32), -1)
    own_segment = lax.dynamic_slice_in_dim(segment, seq * far, length, 0)
    lane = jnp.arange(TILE, dtype=jnp.int32)
    in_head = lane % (TILE // 2)
    matches = segment[:, None] == in_head[None, :]
    aux = jnp.where(
        in_head[None, :] <= pass_count,
        jnp.where(matches, 0.0, MASKED),
        jnp.where((in_head >= 32) & (in_head < 35), -1.0, 0.0)[None, :],
    ).astype(BF)
    one_hot = (own_segment[:, None] == in_head[None, :]).astype(BF)
    spread = (
        (own_segment[:, None] == lane[None, :] % 32) & (lane < 96)[None, :] & (own_segment < pass_count)[:, None]
    ).astype(BF)
    member = (own_segment[None, :] == jnp.arange(pass_count, dtype=jnp.int32)[:, None]).astype(BF)

    def tile_range(segments, tiles, low, high):
        grouped = segments.reshape(tiles, TILE)
        begin = jnp.clip(bounds[grouped[:, 0]], low, high) - low
        end = jnp.clip(bounds[grouped[:, -1] + 1], low, high) - low
        return begin // TILE, (end + TILE - 1) // TILE

    key_lo, key_hi = tile_range(own_segment, length // TILE, window_start, window_start + window)
    query_lo, query_hi = tile_range(segment, window // TILE, own_start, own_start + length)

    queries = (dot(x, query_proj) + query_bias).astype(BF) * jnp.asarray(0.125, BF)
    keys = dot(x_window, key_proj).astype(BF)
    values = (dot(x_window, value_proj) + value_bias).astype(BF)
    context, context_low, qaux = attend(queries, one_hot, keys, values, aux, key_lo, key_hi)

    wide = lambda vector: vector.reshape(1, -1)
    unit1, scale1, hidden_low, active, slope, unit2, scale2, pooled_part = feed(
        context_low, x, member, output_proj, wide(output_bias), wide(first_gain), wide(first_shift),
        expand_proj, wide(expand_bias), shrink_proj, wide(shrink_bias), wide(second_gain), wide(second_shift),
    )

    lengths_wide = lengths.reshape(pass_count, 1).astype(F32)
    pooled = (pooled_part + swap_seq(pooled_part)) / lengths_wide
    inverse = lax.rsqrt(jnp.sum(pooled * pooled, -1, keepdims=True) + 1e-06)
    every = (pooled * inverse).astype(BF)
    for bit in range(int(math.log2(lax.axis_size("dp")))):
        every = join(every, swap_dp(every, bit), 0, (dp >> bit) & 1)
    count = every.shape[0]
    columns = jnp.arange(count, dtype=jnp.int32)
    scores = dot(every, every, ((1,), (1,))) * 100.0
    scores = jnp.where(columns[:, None] == columns[None, :], BIG_NEG, scores)
    log_sums = jax.scipy.special.logsumexp(scores, -1)
    target = columns[None, :] == partners[:, None]
    picked = jnp.sum(jnp.where(target, scores, 0.0), -1)
    own_first = dp * pass_count
    passage_loss = lax.dynamic_slice_in_dim(log_sums - picked, own_first, pass_count, 0)
    weights = jnp.exp(scores - log_sums[:, None]) - target.astype(F32)
    both = lax.dynamic_slice_in_dim(weights, own_first, pass_count, 0) + lax.dynamic_slice_in_dim(
        weights, own_first, pass_count, 1
    ).T
    grad_unit = 100.0 * jnp.dot(both, every.astype(F32), precision=HIGH)
    grad_pooled = (
        inverse * grad_unit - pooled * (inverse**3 * jnp.sum(pooled * grad_unit, -1, keepdims=True))
    ) / lengths_wide
    gap = jnp.zeros((32 - pass_count, features), BF)
    high, middle, low = split3(grad_pooled)
    pooled_parts = jnp.concatenate([high, gap, middle, gap, low, gap, gap, jnp.zeros((pass_count, features), BF)], 0)

    grad_second, grad_shrunk, sums2 = start_back(spread, pooled_parts, unit2, scale2, wide(second_gain))
    grad_shrink = dot(active, grad_shrunk, ((0,), (0,))).astype(BF)
    grad_expanded, grad_first, grad_attended, grad_context, sums1, wide_sums = feed_back(
        grad_second, grad_shrunk, slope, unit1, scale1, shrink_proj, expand_proj, output_proj, wide(first_gain)
    )
    grad_expand = dot(hidden_low, grad_expanded, ((0,), (0,))).astype(BF)
    grad_output = dot(context_low, grad_attended, ((0,), (0,))).astype(BF)
    grad_query, grad_keys, grad_values = attend_back(
        queries, qaux, grad_context, context, keys, values, aux, query_lo, query_hi
    )

    def gather_far(window_grad):
        own = lax.dynamic_slice_in_dim(window_grad, seq * far, length, 0)
        other = swap_seq(lax.dynamic_slice_in_dim(window_grad, (1 - seq) * length, far, 0))
        nothing = jnp.zeros((far, features), BF)
        return (own.astype(F32) + join(other, nothing, 0, 1 - seq).astype(F32)).astype(BF)

    grad_keys = gather_far(grad_keys)
    grad_values = gather_far(grad_values)
    grad_query_proj = dot(x, grad_query, ((0,), (0,))).astype(BF)
    grad_key_proj = dot(x, grad_keys, ((0,), (0,))).astype(BF)
    grad_value_proj = dot(x, grad_values, ((0,), (0,))).astype(BF)
    tokens_grad = (
        grad_first
        + dot(grad_query, query_proj, ((1,), (1,)))
        + dot(grad_keys, key_proj, ((1,), (1,)))
        + dot(grad_values, value_proj, ((1,), (1,)))
    )[None]

    small = jnp.concatenate(
        [
            sums2[:3],
            sums1[:3],
            jnp.sum(grad_query.astype(F32), 0, keepdims=True),
            jnp.sum(grad_values.astype(F32), 0, keepdims=True),
            wide_sums[:1].reshape(-1, features),
        ],
        0,
    )
    small = sum_small(small)
    shrink_total = reduce_all(grad_shrink, 3, 0, 0)
    expand_total = reduce_all(grad_expand, 3, 1, 0)
    output_total = reduce_all(grad_output, 1, 0, 0)
    query_total = reduce_all(grad_query_proj, 1, 0, 0)
    key_total = reduce_all(grad_key_proj, 1, 0, 1)
    value_total = reduce_all(grad_value_proj, 1, 0, 2)
    return (
        passage_loss,
        tokens_grad,
        query_total,
        small[6],
        key_total,
        value_total,
        small[7],
        output_total,
        small[5],
        small[3],
        small[4],
        expand_total,
        small[8:].reshape(-1),
        shrink_total,
        small[2],
        small[0],
        small[1],
    )


def solution(mesh):
    placed = (P("dp", "seq", None), P("dp", None)) + (P(),) * 16
    return jax.shard_map(
        body,
        mesh=mesh,
        in_specs=placed,
        out_specs=(P("dp"), P("dp", "seq", None)) + (P(),) * 15,
        check_vma=False,
    )
```

time: 1440 us -> 588 us (0.41)
  matrix products: 405 us -> 46.2 us
  waiting for transfers between devices: 501 us -> 161 us
  local copies, waits for them, and re-layouts: 364 us -> 47.3 us
  Pallas kernels: 0 us -> 136 us
  starting transfers between devices: 0.24 us -> 104 us
  blocking collectives: 89.5 us -> 0 us
  other arithmetic: 39.4 us -> 83.2 us
    psum x1 -> x0, waiting for transfers between devices: 379 us -> none  [body(): lax.psum((grad_query_proj, grad_query_bias, grad_key_proj, grad_value_pro...]
    dot_general x191 -> x14, matrix products: 405 us -> 46.2 us  [the longest x13 44.5 us: dot(): lax.dot_general(left, right, (over, ((), ())), preferred_element_type=F32)]
    ppermute x0 -> x105, waiting for transfers between devices: none -> 161 us  [the longest x88 160 us: swap_dp(): return lax.ppermute(array, 'dp', [(i, i ^ 1 << bit) for i in range(count)])]
    pallas_call x0 -> x5, Pallas kernels: none -> 136 us  [the longest x1 50 us: attend_back(): pl.pallas_call(attend_back_kernel, grid_spec=pltpu.PrefetchScalarGridSpec...]
    while x374 -> x0, local copies, waits for them, and re-layouts: 123 us -> none
    reduce_scatter x3 -> x0, waiting for transfers between devices: 118 us -> none  [the longest x1 118 us: body(): lax.psum_scatter(spread_terms, 'dp', scatter_dimension=0, tiled=True)]
    ppermute x0 -> x105, starting transfers between devices: none -> 104 us  [the longest x88 87.6 us: swap_dp(): return lax.ppermute(array, 'dp', [(i, i ^ 1 << bit) for i in range(count)])]
    dynamic_slice x169 -> x51, local copies, waits for them, and re-layouts: 75.8 us -> 12.8 us  [the longest x46 7.37 us: pick_half(): return lax.dynamic_slice_in_dim(array, which * half, half, axis)]
  transfers between devices with their start and end apart: 6 -> 105, of which waited for: 3 -> 55; matrix products, arithmetic and copies ran while one was open for 5% -> 21% of each run, Pallas kernels for 0% -> 9%
where the time goes in v1:
time: 588 us; the launch traced here: 582 us
  waiting for transfers between devices  161 us (27%)
  Pallas kernels  136 us (23%)
  starting transfers between devices  104 us (18%)
  other arithmetic  83.2 us (14%)
  local copies, waits for them, and re-layouts  47.3 us (8%)
  matrix products  46.2 us (8%)
    ppermute x88, waiting for transfers between devices, swap_dp(): return lax.ppermute(array, 'dp', [(i, i ^ 1 << bit) for i in range(count)])  160 us
    ppermute x88, starting transfers between devices, swap_dp(): return lax.ppermute(array, 'dp', [(i, i ^ 1 << bit) for i in range(count)])  87.6 us
    pallas_call x1, Pallas kernels, attend_back(): pl.pallas_call(attend_back_kernel, grid_spec=pltpu.PrefetchScalarGridSpec...  50 us
    convert_element_type x6, other arithmetic, reduce_all(): return join(half, swap_seq(half), 0, seq).astype(F32)  45.1 us
    dot_general x13, matrix products, dot(): lax.dot_general(left, right, (over, ((), ())), preferred_element_type=F32)  44.5 us
    pallas_call x1, Pallas kernels, feed(): pl.pallas_call(feed_kernel, grid=(length // rows,), in_specs=[pl.BlockSpe...  32.5 us
    pallas_call x1, Pallas kernels, attend(): pl.pallas_call(attend_kernel, grid_spec=pltpu.PrefetchScalarGridSpec(num_...  24.8 us
    pallas_call x1, Pallas kernels, feed_back(): pl.pallas_call(feed_back_kernel, grid=(length // rows,), in_specs=[pl.Blo...  23.4 us
  transfers between devices with their start and end apart: 105, of which 55 were waited for; matrix products, arithmetic and copies ran while one was open for 21% of the time, Pallas kernels for 9%

profile of v1, /device:TPU:0, one launch (start us, length us, event | category | flops | bytes accessed | tf_op | source)
XLA Modules:
  0.0 581.7 jit_solution(1288780765786474921)
XLA Ops:
  23.6 24.8 %attend.1 = (f32[1024,768]{1,0:T(8,128)S(1)}, bf16[1024,768]{1,0:T(8,128)(2,1)S(1)}, bf16[1024,768]{1,0:T(8,128)(2,1)S(1)}) custom-call(s32[8]{0:T(128)S(1)} %get-tuple-element.102.lo_ref, s32[8]{0:T(128)S(1)} %get-tuple-element.101.hi_ref, bf16[1024,768]{1,0:T(8,128)(2,1)S(1)} %fusion.2.q_ref, bf16[1024,128]{1,0:T(8,128)(2,1)S(1)} %get-tuple-element.92.one_ref, ...), custom_call_target="tpu_custom_call" | custom-call | tf_op jit(solution)/shard_map/attend/pallas_call | solution.py:122
  52.5 32.5 %feed.1 = (bf16[1024,768]{1,0:T(8,128)(2,1)S(1)}, f32[1024,1]{1,0:T(8,128)S(1)}, bf16[1024,768]{1,0:T(8,128)(2,1)S(1)}, bf16[1024,3072]{1,0:T(8,128)(2,1)}, bf16...) custom-call(bf16[1024,768]{1,0:T(8,128)(2,1)} %copy-done.13, ...), custom_call_target="tpu_custom_call" | custom-call | tf_op jit(solution)/shard_map/feed/pallas_call | solution.py:319
  88.9 4.1 collective-permute-start.1
  117.4 6.4 %collective-permute-done.5 = bf16[128,768]{1,0:T(8,128)(2,1)S(1)} collective-permute-done((bf16[128,768]{1,0:T(8,128)(2,1)S(1)}, bf16[128,768]{1,0:T(8,128)(2,1)S(1)}, u32[]{:S(2)}, u32[]{:S(2)}) %collective-permute-start.5) | collective-permute-done | bytes 196640 | tf_op jit(solution)/shard_map/ppermute | solution.py:491
  134.3 5.6 start_back.1
  139.8 8.2 %convolution_convert_fusion = bf16[3072,768]{1,0:T(8,128)(2,1)S(1)} fusion(bf16[1024,3072]{1,0:T(8,128)(2,1)} %get-tuple-element.62, bf16[1024,768]{1,0:T(8,128)(2,1)} %get-tuple-element.45.dy_ref), kind=kOutput, calls=%fused_computation.4 | convolution fusion | flops 4834197504 | bytes 12582912 | tf_op jit(solution)/shard_map/dot_general | solution.py:23
  148.1 23.4 %feed_back.1 = (bf16[1024,3072]{1,0:T(8,128)(2,1)}, f32[1024,768]{1,0:T(8,128)}, bf16[1024,768]{1,0:T(8,128)(2,1)S(1)}, bf16[1024,768]{1,0:T(8,128)(2,1)S(1)}, f...) custom-call(f32[1024,768]{1,0:T(8,128)} %get-tuple-element.44.dr2_ref, bf16[1024,768]{1,0:T(8,128)(2,1)} %get-tuple-element.45.dy_ref, ...), custom_call_target="tpu_custom_call" | custom-call | tf_op jit(solution)/shard_map/feed_back/pallas_call | solution.py:450
  174.3 50.0 %attend_back.1 = (bf16[1024,768]{1,0:T(8,128)(2,1)S(1)}, bf16[1536,768]{1,0:T(8,128)(2,1)S(1)}, bf16[1536,768]{1,0:T(8,128)(2,1)S(1)}) custom-call(s32[12]{0:T(128)S(1)} %get-tuple-element.100.lo_ref, s32[12]{0:T(128)S(1)} %get-tuple-element.99.hi_ref, bf16[1024,768]{1,0:T(8,128)(2,1)S(1)} %copy-done.5, bf16[1024,768]{1,0:T(8,128)(2,1)S(1)} %copy-done.12, ...), custom_call_target="tpu_custom_call" | custom-call | tf_op jit(solution)/shard_map/attend_back/pallas_call | solution.py:219
  226.2 10.1 %collective-permute-start.7 = (bf16[512,768]{1,0:T(8,128)(2,1)}, bf16[512,768]{1,0:T(8,128)(2,1)}, u32[]{:S(2)}, u32[]{:S(2)}) collective-permute-start(bf16[512,768]{1,0:T(8,128)(2,1)} %constant_dynamic-slice_fusion.43), channel_id=1, source_target_pairs={{0,1},{1,0},{2,3},{3,2},{4,5},{5,4},{6,7},{7,6},{8,9},{9,8},{10,11... | collective-permute-start | bytes 2359304 | tf_op jit(solution)/shard_map/ppermute | solution.py:486
  241.3 5.6 convolution_convert_fusion.1
  291.3 5.5 collective-permute-done.10
  296.9 4.3 collective-permute-done.46
  301.2 4.3 collective-permute-done.11
  307.0 4.4 collective-permute-done.47
  311.8 4.6 collective-permute-done.12
  316.6 4.6 collective-permute-done.48
  321.5 4.7 collective-permute-done.13
  326.2 4.3 collective-permute-done.49
  330.6 5.3 collective-permute-done.14
  345.9 5.0 collective-permute-done.34
  357.4 7.0 %collective-permute-done.35 = bf16[96,768]{1,0:T(8,128)(2,1)S(1)} collective-permute-done((bf16[96,768]{1,0:T(8,128)(2,1)S(1)}, bf16[96,768]{1,0:T(8,128)(2,1)S(1)}, u32[]{:S(2)}, u32[]{:S(2)}) %collective-permute-start.35) | collective-permute-done | bytes 147488 | tf_op jit(solution)/shard_map/ppermute | solution.py:491
  364.5 4.3 collective-permute-done.26
  373.6 4.4 collective-permute-done.27
  382.4 4.4 collective-permute-done.28
  391.1 4.8 collective-permute-done.29
  397.0 4.1 collective-permute-done.39
  407.2 6.6 %collective-permute-done.40 = bf16[96,768]{1,0:T(8,128)(2,1)S(1)} collective-permute-done((bf16[96,768]{1,0:T(8,128)(2,1)S(1)}, bf16[96,768]{1,0:T(8,128)(2,1)S(1)}, u32[]{:S(2)}, u32[]{:S(2)}) %collective-permute-start.40) | collective-permute-done | bytes 147488 | tf_op jit(solution)/shard_map/ppermute | solution.py:491
  439.7 6.3 %collective-permute-done.97 = bf16[128,768]{1,0:T(8,128)(2,1)S(1)} collective-permute-done((bf16[128,768]{1,0:T(8,128)(2,1)S(1)}, bf16[128,768]{1,0:T(8,128)(2,1)S(1)}, u32[]{:S(2)}, u32[]{:S(2)}) %collective-permute-start.97) | collective-permute-done | bytes 196640 | tf_op jit(solution)/shard_map/ppermute | solution.py:491
  501.5 6.1 %collective-permute-done.69 = bf16[192,1024]{1,0:T(8,128)(2,1)S(1)} collective-permute-done((bf16[192,1024]{1,0:T(8,128)(2,1)S(1)}, bf16[192,1024]{1,0:T(8,128)(2,1)S(1)}, u32[]{:S(2)}, u32[]{:S(2)}) %collective-permute-start.69) | collective-permute-done | bytes 393248 | tf_op jit(solution)/shard_map/ppermute | solution.py:491
  526.1 5.0 add_bitcast_fusion
  546.0 28.7 %fusion = f32[768,3072]{1,0:T(8,128)} fusion(bf16[384,3072]{1,0:T(8,128)(2,1)} %collective-permute-done.78, bf16[384,1024]{1,0:T(8,128)(2,1)S(1)} %copy-done.32, bf16[384,1024]{1,0:T(8,128)(2,1)S(1)} %copy-done.30, bf16[384,1024]{1,0:T(8,128)(2,1)S(1)} %copy-done.34, pred[]{:T(512)S(6)} %eq.60), kind=kLoop, calls=%fused_computation.7 | loop fusion | flops 42467328 | bytes 14155777 | tf_op jit(solution)/shard_map/convert_element_type | solution.py:538
  574.8 6.5 %fusion.1 = f32[3072,768]{1,0:T(8,128)} fusion(bf16[1536,768]{1,0:T(8,128)(2,1)} %collective-permute-done.104, bf16[512,768]{1,0:T(8,128)(2,1)S(1)} %copy-done.38, bf16[512,768]{1,0:T(8,128)(2,1)S(1)} %copy-done.36, bf16[512,768]{1,0:T(8,128)(2,1)S(1)} %copy-done.40, pred[]{:T(512)S(6)} %eq.60), kind=kLoop, calls=%fused_computation.9 | loop fusion | flops 42467328 | bytes 14155777 | tf_op jit(solution)/shard_map/convert_element_type | solution.py:538
  (576 shorter events, 272.5 us)
Async XLA Ops:
  2.9 13.3 %collective-permute-start = (bf16[512,768]{1,0:T(8,128)(2,1)}, bf16[512,768]{1,0:T(8,128)(2,1)}, u32[]{:S(2)}, u32[]{:S(2)}) collective-permute-start(bf16[512,768]{1,0:T(8,128)(2,1)} %dynamic-slice_bitcast_fusion), channel_id=1, source_target_pairs={{0,1},{1,0},{2,3},{3,2},{4,5},{5,4},{6,7},{7,6},{8,9},{9,8},{10,11... | collective-permute-start | bytes 2359304 | tf_op jit(solution)/shard_map/ppermute | solution.py:486
  113.5 10.3 %collective-permute-start.5 = (bf16[128,768]{1,0:T(8,128)(2,1)S(1)}, bf16[128,768]{1,0:T(8,128)(2,1)S(1)}, u32[]{:S(2)}, u32[]{:S(2)}) collective-permute-start(bf16[128,768]{1,0:T(8,128)(2,1)S(1)} %maximum_select_fusion.30), channel_id=1, source_target_pairs={{0,16},{2,18},{4,20},{6,22},{8,24},{10,26},{12,28},{14,30},{16,0},... | collective-permute-start | bytes 589832 | tf_op jit(solution)/shard_map/ppermute | solution.py:491
  174.0 80.5 %collective-permute-start.43 = (bf16[384,768]{1,0:T(8,128)(2,1)}, bf16[384,768]{1,0:T(8,128)(2,1)}, u32[]{:S(2)}, u32[]{:S(2)}) collective-permute-start(bf16[384,768]{1,0:T(8,128)(2,1)} %constant_dynamic-slice_fusion.30), channel_id=1, source_target_pairs={{0,1},{1,0},{2,3},{3,2},{4,5},{5,4},{6,7},{7,6},{8,9},{9,8},{10,11... | collective-permute-start | bytes 1769480 | tf_op jit(solution)/shard_map/ppermute | solution.py:486
  226.2 34.9 %collective-permute-start.7 = (bf16[512,768]{1,0:T(8,128)(2,1)}, bf16[512,768]{1,0:T(8,128)(2,1)}, u32[]{:S(2)}, u32[]{:S(2)}) collective-permute-start(bf16[512,768]{1,0:T(8,128)(2,1)} %constant_dynamic-slice_fusion.43), channel_id=1, source_target_pairs={{0,1},{1,0},{2,3},{3,2},{4,5},{5,4},{6,7},{7,6},{8,9},{9,8},{10,11... | collective-permute-start | bytes 2359304 | tf_op jit(solution)/shard_map/ppermute | solution.py:486
  236.3 35.4 %collective-permute-start.6 = (bf16[512,768]{1,0:T(8,128)(2,1)}, bf16[512,768]{1,0:T(8,128)(2,1)}, u32[]{:S(2)}, u32[]{:S(2)}) collective-permute-start(bf16[512,768]{1,0:T(8,128)(2,1)} %constant_dynamic-slice_fusion.44), channel_id=1, source_target_pairs={{0,1},{1,0},{2,3},{3,2},{4,5},{5,4},{6,7},{7,6},{8,9},{9,8},{10,11... | collective-permute-start | bytes 2359304 | tf_op jit(solution)/shard_map/ppermute | solution.py:486
  239.1 19.0 %collective-permute-start.8 = (bf16[384,768]{1,0:T(8,128)(2,1)}, bf16[384,768]{1,0:T(8,128)(2,1)}, u32[]{:S(2)}, u32[]{:S(2)}) collective-permute-start(bf16[384,768]{1,0:T(8,128)(2,1)} %dynamic-slice_bitcast_fusion.3), channel_id=1, source_target_pairs={{0,1},{1,0},{2,3},{3,2},{4,5},{5,4},{6,7},{7,6},{8,9},{9,8},{10,11... | collective-permute-start | bytes 1769480 | tf_op jit(solution)/shard_map/ppermute | solution.py:486
  241.3 172.6 %collective-permute-start.79 = (bf16[1536,768]{1,0:T(8,128)(2,1)}, bf16[1536,768]{1,0:T(8,128)(2,1)}, u32[]{:S(2)}, u32[]{:S(2)}) collective-permute-start(bf16[1536,768]{1,0:T(8,128)(2,1)} %constant_dynamic-slice_fusion.12), channel_id=1, source_target_pairs={{0,1},{1,0},{2,3},{3,2},{4,5},{5,4},{6,7},{7,6},{8,9},{9,8},{10,11... | collective-permute-start | bytes 7077896 | tf_op jit(solution)/shard_map/ppermute | solution.py:486
  254.4 164.9 %collective-permute-start.53 = (bf16[384,3072]{1,0:T(8,128)(2,1)}, bf16[384,3072]{1,0:T(8,128)(2,1)}, u32[]{:S(2)}, u32[]{:S(2)}) collective-permute-start(bf16[384,3072]{1,0:T(8,128)(2,1)} %constant_dynamic-slice_fusion.25), channel_id=1, source_target_pairs={{0,1},{1,0},{2,3},{3,2},{4,5},{5,4},{6,7},{7,6},{8,9},{9,8},{10,11... | collective-permute-start | bytes 7077896 | tf_op jit(solution)/shard_map/ppermute | solution.py:486
  258.1 23.9 %collective-permute-start.44 = (bf16[192,768]{1,0:T(8,128)(2,1)}, bf16[192,768]{1,0:T(8,128)(2,1)}, u32[]{:S(2)}, u32[]{:S(2)}) collective-permute-start(bf16[192,768]{1,0:T(8,128)(2,1)} %constant_dynamic-slice_fusion.29), channel_id=1, source_target_pairs={{0,2},{2,0},{4,6},{6,4},{8,10},{10,8},{12,14},{14,12},{16,18},{18,... | collective-permute-start | bytes 884744 | tf_op jit(solution)/shard_map/ppermute | solution.py:491
  261.0 22.2 %collective-permute-start.9 = (bf16[192,768]{1,0:T(8,128)(2,1)}, bf16[192,768]{1,0:T(8,128)(2,1)}, u32[]{:S(2)}, u32[]{:S(2)}) collective-permute-start(bf16[192,768]{1,0:T(8,128)(2,1)} %constant_dynamic-slice_fusion.42), channel_id=1, source_target_pairs={{0,2},{2,0},{4,6},{6,4},{8,10},{10,8},{12,14},{14,12},{16,18},{18,... | collective-permute-start | bytes 884744 | tf_op jit(solution)/shard_map/ppermute | solution.py:491
  282.0 54.4 %collective-permute-start.23 = (bf16[384,768]{1,0:T(8,128)(2,1)S(1)}, bf16[384,768]{1,0:T(8,128)(2,1)S(1)}, u32[]{:S(2)}, u32[]{:S(2)}) collective-permute-start(bf16[384,768]{1,0:T(8,128)(2,1)S(1)} %dynamic-slice_bitcast_fusion.2), channel_id=1, source_target_pairs={{0,1},{1,0},{2,3},{3,2},{4,5},{5,4},{6,7},{7,6},{8,9},{9,8},{10,11... | collective-permute-start | bytes 1769480 | tf_op jit(solution)/shard_map/ppermute | solution.py:486
  290.5 47.8 %collective-permute-start.33 = (bf16[384,768]{1,0:T(8,128)(2,1)S(1)}, bf16[384,768]{1,0:T(8,128)(2,1)S(1)}, u32[]{:S(2)}, u32[]{:S(2)}) collective-permute-start(bf16[384,768]{1,0:T(8,128)(2,1)S(1)} %dynamic-slice_bitcast_fusion.1), channel_id=1, source_target_pairs={{0,1},{1,0},{2,3},{3,2},{4,5},{5,4},{6,7},{7,6},{8,9},{9,8},{10,11... | collective-permute-start | bytes 1769480 | tf_op jit(solution)/shard_map/ppermute | solution.py:486
  341.0 179.6 %collective-permute-start.22 = (f32[12,768]{1,0:T(8,128)S(1)}, f32[12,768]{1,0:T(8,128)S(1)}, u32[]{:S(2)}, u32[]{:S(2)}) collective-permute-start(f32[12,768]{1,0:T(8,128)S(1)} %add.560), channel_id=1, source_target_pairs={{0,16},{2,18},{4,20},{6,22},{8,24},{10,26},{12,28},{14,30},{16,0},... | collective-permute-start | bytes 110600 | tf_op jit(solution)/shard_map/ppermute | solution.py:491
  352.5 49.7 %collective-permute-start.16 = (bf16[192,768]{1,0:T(8,128)(2,1)S(1)}, bf16[192,768]{1,0:T(8,128)(2,1)S(1)}, u32[]{:S(2)}, u32[]{:S(2)}) collective-permute-start(bf16[192,768]{1,0:T(8,128)(2,1)S(1)} %maximum_select_fusion.26), channel_id=1, source_target_pairs={{0,2},{2,0},{4,6},{6,4},{8,10},{10,8},{12,14},{14,12},{16,18},{18,... | collective-permute-start | bytes 884744 | tf_op jit(solution)/shard_map/ppermute | solution.py:491
  402.2 11.6 %collective-permute-start.40 = (bf16[96,768]{1,0:T(8,128)(2,1)S(1)}, bf16[96,768]{1,0:T(8,128)(2,1)S(1)}, u32[]{:S(2)}, u32[]{:S(2)}) collective-permute-start(bf16[96,768]{1,0:T(8,128)(2,1)S(1)} %maximum_select_fusion.39), channel_id=1, source_target_pairs={{0,16},{2,18},{4,20},{6,22},{8,24},{10,26},{12,28},{14,30},{16,0},... | collective-permute-start | bytes 442376 | tf_op jit(solution)/shard_map/ppermute | solution.py:491
  418.1 9.4 %collective-permute-start.96 = (bf16[256,768]{1,0:T(8,128)(2,1)S(1)}, bf16[256,768]{1,0:T(8,128)(2,1)S(1)}, u32[]{:S(2)}, u32[]{:S(2)}) collective-permute-start(bf16[256,768]{1,0:T(8,128)(2,1)S(1)} %constant_dynamic-slice_fusion.3), channel_id=1, source_target_pairs={{0,8},{2,10},{4,12},{6,14},{8,0},{10,2},{12,4},{14,6},{16,24},{18,... | collective-permute-start | bytes 1179656 | tf_op jit(solution)/shard_map/ppermute | solution.py:491
  418.2 13.0 %collective-permute-start.80 = (bf16[256,768]{1,0:T(8,128)(2,1)S(1)}, bf16[256,768]{1,0:T(8,128)(2,1)S(1)}, u32[]{:S(2)}, u32[]{:S(2)}) collective-permute-start(bf16[256,768]{1,0:T(8,128)(2,1)S(1)} %constant_dynamic-slice_fusion.11), channel_id=1, source_target_pairs={{0,2},{2,0},{4,6},{6,4},{8,10},{10,8},{12,14},{14,12},{16,18},{18,... | collective-permute-start | bytes 1179656 | tf_op jit(solution)/shard_map/ppermute | solution.py:491
  424.5 10.6 %collective-permute-start.70 = (bf16[192,1024]{1,0:T(8,128)(2,1)S(1)}, bf16[192,1024]{1,0:T(8,128)(2,1)S(1)}, u32[]{:S(2)}, u32[]{:S(2)}) collective-permute-start(bf16[192,1024]{1,0:T(8,128)(2,1)S(1)} %constant_dynamic-slice_fusion.16), channel_id=1, source_target_pairs={{0,8},{2,10},{4,12},{6,14},{8,0},{10,2},{12,4},{14,6},{16,24},{18,... | collective-permute-start | bytes 1179656 | tf_op jit(solution)/shard_map/ppermute | solution.py:491
  431.2 14.8 %collective-permute-start.97 = (bf16[128,768]{1,0:T(8,128)(2,1)S(1)}, bf16[128,768]{1,0:T(8,128)(2,1)S(1)}, u32[]{:S(2)}, u32[]{:S(2)}) collective-permute-start(bf16[128,768]{1,0:T(8,128)(2,1)S(1)} %constant_dynamic-slice_fusion.2), channel_id=1, source_target_pairs={{0,16},{2,18},{4,20},{6,22},{8,24},{10,26},{12,28},{14,30},{16,0},... | collective-permute-start | bytes 589832 | tf_op jit(solution)/shard_map/ppermute | solution.py:491
  435.1 11.3 %collective-permute-start.81 = (bf16[128,768]{1,0:T(8,128)(2,1)S(1)}, bf16[128,768]{1,0:T(8,128)(2,1)S(1)}, u32[]{:S(2)}, u32[]{:S(2)}) collective-permute-start(bf16[128,768]{1,0:T(8,128)(2,1)S(1)} %constant_dynamic-slice_fusion.10), channel_id=1, source_target_pairs={{0,4},{2,6},{4,0},{6,2},{8,12},{10,14},{12,8},{14,10},{16,20},{18,... | collective-permute-start | bytes 589832 | tf_op jit(solution)/shard_map/ppermute | solution.py:491
  435.5 11.1 %collective-permute-start.63 = (bf16[96,1024]{1,0:T(8,128)(2,1)S(1)}, bf16[96,1024]{1,0:T(8,128)(2,1)S(1)}, u32[]{:S(2)}, u32[]{:S(2)}) collective-permute-start(bf16[96,1024]{1,0:T(8,128)(2,1)S(1)} %constant_dynamic-slice_fusion.19), channel_id=1, source_target_pairs={{0,2},{2,0},{4,6},{6,4},{8,10},{10,8},{12,14},{14,12},{16,18},{18,... | collective-permute-start | bytes 589832 | tf_op jit(solution)/shard_map/ppermute | solution.py:491
  437.4 10.7 %collective-permute-start.71 = (bf16[96,1024]{1,0:T(8,128)(2,1)S(1)}, bf16[96,1024]{1,0:T(8,128)(2,1)S(1)}, u32[]{:S(2)}, u32[]{:S(2)}) collective-permute-start(bf16[96,1024]{1,0:T(8,128)(2,1)S(1)} %constant_dynamic-slice_fusion.15), channel_id=1, source_target_pairs={{0,16},{2,18},{4,20},{6,22},{8,24},{10,26},{12,28},{14,30},{16,0},... | collective-permute-start | bytes 589832 | tf_op jit(solution)/shard_map/ppermute | solution.py:491
  451.7 9.9 %collective-permute-start.72 = (bf16[48,1024]{1,0:T(8,128)(2,1)S(1)}, bf16[48,1024]{1,0:T(8,128)(2,1)S(1)}, u32[]{:S(2)}, u32[]{:S(2)}) collective-permute-start(bf16[48,1024]{1,0:T(8,128)(2,1)S(1)} %constant_dynamic-slice_fusion.14), channel_id=1, source_target_pairs={{0,2},{2,0},{4,6},{6,4},{8,10},{10,8},{12,14},{14,12},{16,18},{18,... | collective-permute-start | bytes 294920 | tf_op jit(solution)/shard_map/ppermute | solution.py:491
  457.3 9.7 %collective-permute-start.99 = (bf16[32,768]{1,0:T(8,128)(2,1)S(1)}, bf16[32,768]{1,0:T(8,128)(2,1)S(1)}, u32[]{:S(2)}, u32[]{:S(2)}) collective-permute-start(bf16[32,768]{1,0:T(8,128)(2,1)S(1)} %constant_dynamic-slice_fusion), channel_id=1, source_target_pairs={{0,4},{2,6},{4,0},{6,2},{8,12},{10,14},{12,8},{14,10},{16,20},{18,... | collective-permute-start | bytes 147464 | tf_op jit(solution)/shard_map/ppermute | solution.py:491
  485.0 15.4 %collective-permute-start.102 = (bf16[128,768]{1,0:T(8,128)(2,1)S(1)}, bf16[128,768]{1,0:T(8,128)(2,1)S(1)}, u32[]{:S(2)}, u32[]{:S(2)}) collective-permute-start(bf16[128,768]{1,0:T(8,128)(2,1)S(1)} %maximum_select_fusion.36), channel_id=1, source_target_pairs={{0,16},{2,18},{4,20},{6,22},{8,24},{10,26},{12,28},{14,30},{16,0},... | collective-permute-start | bytes 589832 | tf_op jit(solution)/shard_map/ppermute | solution.py:491
  487.2 14.1 %collective-permute-start.86 = (bf16[128,768]{1,0:T(8,128)(2,1)S(1)}, bf16[128,768]{1,0:T(8,128)(2,1)S(1)}, u32[]{:S(2)}, u32[]{:S(2)}) collective-permute-start(bf16[128,768]{1,0:T(8,128)(2,1)S(1)} %maximum_select_fusion.34), channel_id=1, source_target_pairs={{0,4},{2,6},{4,0},{6,2},{8,12},{10,14},{12,8},{14,10},{16,20},{18,... | collective-permute-start | bytes 589832 | tf_op jit(solution)/shard_map/ppermute | solution.py:491
  501.3 37.3 %collective-permute-start.52 = (bf16[384,768]{1,0:T(8,128)(2,1)}, bf16[384,768]{1,0:T(8,128)(2,1)}, u32[]{:S(2)}, u32[]{:S(2)}) collective-permute-start(bf16[384,768]{1,0:T(8,128)(2,1)} %maximum_select_fusion.16), channel_id=1, source_target_pairs={{0,1},{1,0},{2,3},{3,2},{4,5},{5,4},{6,7},{7,6},{8,9},{9,8},{10,11... | collective-permute-start | bytes 1769480 | tf_op jit(solution)/shard_map/ppermute | solution.py:486
  515.4 29.8 %collective-permute-start.78 = (bf16[384,3072]{1,0:T(8,128)(2,1)}, bf16[384,3072]{1,0:T(8,128)(2,1)}, u32[]{:S(2)}, u32[]{:S(2)}) collective-permute-start(bf16[384,3072]{1,0:T(8,128)(2,1)} %pad_maximum_fusion), channel_id=1, source_target_pairs={{0,1},{1,0},{2,3},{3,2},{4,5},{5,4},{6,7},{7,6},{8,9},{9,8},{10,11... | collective-permute-start | bytes 7077896 | tf_op jit(solution)/shard_map/ppermute | solution.py:486
  516.3 18.3 %collective-permute-start.17 = (bf16[384,768]{1,0:T(8,128)(2,1)}, bf16[384,768]{1,0:T(8,128)(2,1)}, u32[]{:S(2)}, u32[]{:S(2)}) collective-permute-start(bf16[384,768]{1,0:T(8,128)(2,1)} %maximum_select_fusion.13), channel_id=1, source_target_pairs={{0,1},{1,0},{2,3},{3,2},{4,5},{5,4},{6,7},{7,6},{8,9},{9,8},{10,11... | collective-permute-start | bytes 1769480 | tf_op jit(solution)/shard_map/ppermute | solution.py:486
  520.7 10.6 %collective-permute-start.31 = (bf16[192,768]{1,0:T(8,128)(2,1)S(1)}, bf16[192,768]{1,0:T(8,128)(2,1)S(1)}, u32[]{:S(2)}, u32[]{:S(2)}) collective-permute-start(bf16[192,768]{1,0:T(8,128)(2,1)S(1)} %maximum_select_fusion.27), channel_id=1, source_target_pairs={{0,4},{2,6},{4,0},{6,2},{8,12},{10,14},{12,8},{14,10},{16,20},{18,... | collective-permute-start | bytes 884744 | tf_op jit(solution)/shard_map/ppermute | solution.py:491
  526.1 48.7 %collective-permute-start.104 = (bf16[1536,768]{1,0:T(8,128)(2,1)}, bf16[1536,768]{1,0:T(8,128)(2,1)}, u32[]{:S(2)}, u32[]{:S(2)}) collective-permute-start(bf16[1536,768]{1,0:T(8,128)(2,1)} %pad_maximum_fusion.1), channel_id=1, source_target_pairs={{0,1},{1,0},{2,3},{3,2},{4,5},{5,4},{6,7},{7,6},{8,9},{9,8},{10,11... | collective-permute-start | bytes 7077896 | tf_op jit(solution)/shard_map/ppermute | solution.py:486
  532.0 9.9 %collective-permute-start.42 = (bf16[384,768]{1,0:T(8,128)(2,1)S(1)}, bf16[384,768]{1,0:T(8,128)(2,1)S(1)}, u32[]{:S(2)}, u32[]{:S(2)}) collective-permute-start(bf16[384,768]{1,0:T(8,128)(2,1)S(1)} %maximum_select_fusion.15), channel_id=1, source_target_pairs={{0,1},{1,0},{2,3},{3,2},{4,5},{5,4},{6,7},{7,6},{8,9},{9,8},{10,11... | collective-permute-start | bytes 1769480 | tf_op jit(solution)/shard_map/ppermute | solution.py:486
  (153 other events, 1563.9 us)

commit v2 on v1

v2 whole, which is shorter than its diff:
```python
import functools
import math

import jax
import jax.numpy as jnp
from jax import lax
from jax.experimental import pallas as pl
from jax.experimental.pallas import tpu as pltpu
from jax.sharding import PartitionSpec as P

HEADS = 12
EPS_NORM = 1e-12
BIG_NEG = -1000000000.0
HIGH = lax.Precision.HIGHEST
BF = jnp.bfloat16
F32 = jnp.float32
TILE = 128
MASKED = -float(2**30)
BIAS_O, GAIN_1, SHIFT_1, BIAS_S, GAIN_2, SHIFT_2, BIAS_Q, BIAS_V, BIAS_E = range(9)
VMEM_MIB = 1 << 20


def dot(left, right, over=((1,), (0,))):
    return lax.dot_general(left, right, (over, ((), ())), preferred_element_type=F32)


def split3(value):
    high = value.astype(BF)
    rest = value - high.astype(F32)
    middle = rest.astype(BF)
    low = (rest - middle.astype(F32)).astype(BF)
    return high, middle, low


def split_lanes(pair):
    row = lax.broadcasted_iota(jnp.int32, (TILE, 1), 0)
    first = jnp.where(row < TILE // 2, 1.0, 0.0).astype(BF)
    second = jnp.where(row < TILE // 2, 0.0, 1.0).astype(BF)
    return jnp.concatenate([pair * first, pair * second], 1)


def split_rows(pair):
    lane = lax.broadcasted_iota(jnp.int32, (1, TILE), 1)
    first = jnp.where(lane < TILE // 2, 1.0, 0.0).astype(BF)
    second = jnp.where(lane < TILE // 2, 0.0, 1.0).astype(BF)
    return jnp.concatenate([pair * first, pair * second], 0)


def lanes_to_rows(both):
    return jnp.concatenate([both[:, :TILE], both[:, TILE:]], 0)


def attend_kernel(
    lo_ref, hi_ref, qt_ref, onet_ref, k_ref, vt_ref, aux_ref, c_ref, ct_ref, ctb_ref, lse_ref, s_scr, q_scr, m_scr, o_scr
):
    lo, hi = lo_ref[pl.program_id(0)], hi_ref[pl.program_id(0)]
    pairs = k_ref.shape[1] // TILE
    m_scr[...] = jnp.full(m_scr.shape, 2.0 * MASKED, F32)
    o_scr[...] = jnp.zeros(o_scr.shape, F32)
    one = onet_ref[...]
    for j in range(pairs):
        q_scr[j, :TILE, :] = split_lanes(qt_ref[j * TILE : (j + 1) * TILE, :])
        q_scr[j, TILE:, :] = jnp.concatenate([one, one], 1)
    extra = o_scr.shape[1] - TILE
    row = lax.broadcasted_iota(jnp.int32, (extra, 2 * TILE), 0)
    lane = lax.broadcasted_iota(jnp.int32, (extra, 2 * TILE), 1)
    ones = jnp.where(row == lane // TILE, 1.0, 0.0).astype(BF)

    count = (hi - lo + 1) // 2
    lo = jnp.minimum(lo, k_ref.shape[0] // TILE - 2 * count)

    def scores(step, carry):
        start = pl.multiple_of((lo + 2 * step) * TILE, TILE)
        for half in range(2):
            rows = pl.ds(pl.multiple_of(start + half * TILE, TILE), TILE)
            aux = aux_ref[rows, :]
            for j in range(pairs):
                keys = jnp.concatenate([k_ref[rows, j * TILE : (j + 1) * TILE], aux], 1)
                s = dot(keys, q_scr[j])
                s_scr[2 * step + half, j] = s
                m_scr[j] = jnp.maximum(m_scr[j], jnp.max(s.reshape(TILE // 8, 8, 2 * TILE), 0))
        return carry

    lax.fori_loop(0, count, scores, 0)
    for j in range(pairs):
        m_scr[j] = jnp.broadcast_to(jnp.max(m_scr[j], 0, keepdims=True), (8, 2 * TILE))

    def weigh(step, carry):
        start = pl.multiple_of((lo + 2 * step) * TILE, TILE)
        for j in range(pairs):
            values, weights = [], []
            for half in range(2):
                cols = pl.ds(pl.multiple_of(start + half * TILE, TILE), TILE)
                p = jnp.exp(s_scr[2 * step + half, j] - m_scr[j, 0:1, :]).astype(BF)
                values.append(
                    jnp.concatenate([split_lanes(vt_ref[j * TILE : (j + 1) * TILE, cols]), ones], 0)
                )
                weights.append(lanes_to_rows(p))
            o_scr[j] += dot(jnp.concatenate(values, 1), jnp.concatenate(weights, 0))
        return carry

    lax.fori_loop(0, count, weigh, 0)
    half = TILE // 2
    for j in range(pairs):
        cols = slice(j * TILE, (j + 1) * TILE)
        total = o_scr[j, TILE : TILE + 2, :]
        inverse = 1.0 / total
        ct = jnp.concatenate(
            [o_scr[j, :half, :] * inverse[0:1], o_scr[j, half:TILE, :] * inverse[1:2]], 0
        )
        ct_ref[cols, :] = ct
        ctb_ref[cols, :] = ct.astype(BF)
        c_ref[:, cols] = ct.T.astype(BF)
        top = jnp.concatenate([m_scr[j, 0:1, :TILE], m_scr[j, 0:1, TILE:]], 0)
        lse_ref[2 * j : 2 * j + 2, :] = top + jnp.log(total)


def attend(queries_t, one_t, keys, values_t, aux, lo, hi):
    features, length = queries_t.shape
    window = keys.shape[0]
    pairs = features // TILE
    row = lambda i, *_: (i, 0)
    col = lambda i, *_: (0, i)
    whole = lambda i, *_: (0, 0)
    return pl.pallas_call(
        attend_kernel,
        grid_spec=pltpu.PrefetchScalarGridSpec(
            num_scalar_prefetch=2,
            grid=(length // TILE,),
            in_specs=[
                pl.BlockSpec((features, TILE), col),
                pl.BlockSpec((TILE, TILE), col),
                pl.BlockSpec((window, features), whole),
                pl.BlockSpec((features, window), whole),
                pl.BlockSpec((window, TILE), whole),
            ],
            out_specs=[
                pl.BlockSpec((TILE, features), row),
                pl.BlockSpec((features, TILE), col),
                pl.BlockSpec((features, TILE), col),
                pl.BlockSpec((2 * pairs, TILE), col),
            ],
            scratch_shapes=[
                pltpu.VMEM((window // TILE, pairs, TILE, 2 * TILE), F32),
                pltpu.VMEM((pairs, 2 * TILE, 2 * TILE), BF),
                pltpu.VMEM((pairs, 8, 2 * TILE), F32),
                pltpu.VMEM((pairs, TILE + 16, TILE), F32),
            ],
        ),
        out_shape=[
            jax.ShapeDtypeStruct((length, features), BF),
            jax.ShapeDtypeStruct((features, length), F32),
            jax.ShapeDtypeStruct((features, length), BF),
            jax.ShapeDtypeStruct((2 * pairs, length), F32),
        ],
        compiler_params=pltpu.CompilerParams(vmem_limit_bytes=60 * VMEM_MIB),
        name="attend",
    )(lo, hi, queries_t, one_t, keys, values_t, aux)


def attend_back_kernel(
    kt_ref, qt_list_ref, count_ref, q_ref, qt_ref, dc_ref, dct_ref, onet_ref, lse_ref, delta_ref, k_ref, keys_t_ref,
    v_ref, aux_ref, dq_ref, dk_ref, dv_ref, dqt_scr, dk_scr, dv_scr,
):
    pairs = q_ref.shape[1] // TILE
    dqt_scr[...] = jnp.zeros(dqt_scr.shape, F32)
    dk_scr[...] = jnp.zeros(dk_scr.shape, F32)
    dv_scr[...] = jnp.zeros(dv_scr.shape, F32)

    def tile(n):
        krows = pl.ds(pl.multiple_of(kt_ref[n] * TILE, TILE), TILE)
        rows = pl.ds(pl.multiple_of(qt_list_ref[n] * TILE, TILE), TILE)
        one = onet_ref[:, rows]
        ones = jnp.concatenate([one, one], 1)
        aux = aux_ref[krows, :]
        for j in range(pairs):
            cols = slice(j * TILE, (j + 1) * TILE)
            keys = jnp.concatenate([k_ref[krows, cols], aux], 1)
            queries_t = jnp.concatenate([split_lanes(qt_ref[cols, rows]), ones], 0)
            lse = jnp.concatenate([lse_ref[2 * j : 2 * j + 1, rows], lse_ref[2 * j + 1 : 2 * j + 2, rows]], 1)
            p = jnp.exp(dot(keys, queries_t) - lse)
            delta = jnp.concatenate([delta_ref[2 * j : 2 * j + 1, rows], delta_ref[2 * j + 1 : 2 * j + 2, rows]], 1)
            ds = (p * (dot(v_ref[krows, cols], split_lanes(dct_ref[cols, rows])) - delta)).astype(BF)
            dv_scr[krows, cols] += dot(p.astype(BF), split_rows(dc_ref[rows, cols]))
            dk_scr[krows, cols] += dot(ds, split_rows(q_ref[rows, cols]))
            dqt_scr[cols, rows] += dot(split_lanes(keys_t_ref[cols, krows]), lanes_to_rows(ds))

    count = count_ref[0]

    def two(step, carry):
        tile(2 * step)
        tile(2 * step + 1)
        return carry

    lax.fori_loop(0, count // 2, two, 0)

    @pl.when(count % 2 == 1)
    def _():
        tile(count - 1)

    dk_ref[...] = dk_scr[...].astype(BF)
    dv_ref[...] = dv_scr[...].astype(BF)
    for i in range(q_ref.shape[0] // TILE):
        for j in range(pairs):
            block = dqt_scr[j * TILE : (j + 1) * TILE, i * TILE : (i + 1) * TILE] * 0.125
            dq_ref[i * TILE : (i + 1) * TILE, j * TILE : (j + 1) * TILE] = block.T.astype(BF)


def attend_back(part, parts, pair_list, queries, queries_t, grads, grads_t, one_t, lse, delta, keys, keys_t, values, aux):
    length, features = queries.shape
    window = keys.shape[0]
    own = features // parts
    heads = lse.shape[0] // parts
    tall = pl.BlockSpec((length, own), lambda i, *_: (0, part))
    flat = pl.BlockSpec((own, length), lambda i, *_: (part, 0))
    tall_window = pl.BlockSpec((window, own), lambda i, *_: (0, part))
    rows = pl.BlockSpec((None, heads, length), lambda i, *_: (part, 0, 0))
    first = lambda i, *_: (0, 0)
    return pl.pallas_call(
        attend_back_kernel,
        grid_spec=pltpu.PrefetchScalarGridSpec(
            num_scalar_prefetch=3,
            grid=(1,),
            in_specs=[
                tall,
                flat,
                tall,
                flat,
                pl.BlockSpec((TILE, length), first),
                rows,
                rows,
                tall_window,
                pl.BlockSpec((own, window), lambda i, *_: (part, 0)),
                tall_window,
                pl.BlockSpec((window, TILE), first),
            ],
            out_specs=[
                pl.BlockSpec((length, own), first),
                pl.BlockSpec((window, own), first),
                pl.BlockSpec((window, own), first),
            ],
            scratch_shapes=[
                pltpu.VMEM((own, length), F32),
                pltpu.VMEM((window, own), F32),
                pltpu.VMEM((window, own), F32),
            ],
        ),
        out_shape=[
            jax.ShapeDtypeStruct((length, own), BF),
            jax.ShapeDtypeStruct((window, own), BF),
            jax.ShapeDtypeStruct((window, own), BF),
        ],
        compiler_params=pltpu.CompilerParams(vmem_limit_bytes=60 * VMEM_MIB),
        name="attend_back",
    )(
        *pair_list, queries, queries_t, grads, grads_t, one_t, lse.reshape(parts, heads, length),
        delta.reshape(parts, heads, length), keys, keys_t, values, aux,
    )


def setup_kernel(
    lengths_ref, seq_ref, aux_ref, onet_ref, spread_ref, lo_ref, hi_ref, kt_ref, qt_ref, count_ref
):
    window, length = aux_ref.shape[0], spread_ref.shape[0]
    far = window - length
    seq = seq_ref[0]
    passages = lengths_ref.shape[1]
    ends, total = [], jnp.int32(0)
    for p in range(passages):
        total = total + lengths_ref[0, p]
        ends.append(total)
    window_start, own_start = seq * far, seq * length

    def segments(positions):
        found = jnp.zeros(positions.shape, jnp.int32)
        for end in ends:
            found = found + jnp.where(positions >= end, 1, 0)
        return found

    lane = lax.broadcasted_iota(jnp.int32, (TILE, TILE), 1)
    row = lax.broadcasted_iota(jnp.int32, (TILE, TILE), 0)

    def window_tile(i, carry):
        rows = pl.ds(pl.multiple_of(i * TILE, TILE), TILE)
        found = segments(window_start + i * TILE + row)
        apart = jnp.where((found != lane) & (lane <= passages), MASKED, 0.0)
        aux_ref[rows, :] = apart.astype(BF)
        return carry

    lax.fori_loop(0, window // TILE, window_tile, 0)

    def own_tile(i, carry):
        rows = pl.ds(pl.multiple_of(i * TILE, TILE), TILE)
        found = segments(own_start + i * TILE + row)
        same = (found == lane % 32) & (lane < 96) & (found < passages)
        spread_ref[rows, :] = jnp.where(same, 1.0, 0.0).astype(BF)
        found = segments(own_start + i * TILE + lane[:8])
        one = jnp.where(jnp.broadcast_to(found[:1], (TILE, TILE)) == row, 1.0, 0.0)
        onet_ref[:, rows] = one.astype(BF)
        return carry

    lax.fori_loop(0, length // TILE, own_tile, 0)

    def reach(first, low, high):
        begin, end = jnp.int32(0), jnp.int32(2 * length)
        for stop in ends:
            begin = jnp.where(stop <= first, stop, begin)
        for stop in reversed(ends):
            end = jnp.where(stop > first + TILE - 1, stop, end)
        begin = jnp.clip(begin, low, high) - low
        end = jnp.clip(end, low, high) - low
        return begin // TILE, (end + TILE - 1) // TILE

    for i in range(length // TILE):
        lo_ref[i], hi_ref[i] = reach(own_start + i * TILE, window_start, window_start + window)
    count = jnp.int32(0)
    for t in range(window // TILE):
        low, high = reach(window_start + t * TILE, own_start, own_start + length)

        def put(i, count):
            kt_ref[count] = t
            qt_ref[count] = i
            return count + 1

        count = lax.fori_loop(low, high, put, count)
    count_ref[0] = count


def setup(lengths, seq, length, window):
    tiles, window_tiles = length // TILE, window // TILE
    smem = pl.BlockSpec(memory_space=pltpu.SMEM)
    vmem = pl.BlockSpec(memory_space=pltpu.VMEM)
    number = lambda n: jax.ShapeDtypeStruct((n,), jnp.int32)
    return pl.pallas_call(
        setup_kernel,
        in_specs=[smem, smem],
        out_specs=[vmem] * 3 + [smem] * 5,
        out_shape=[
            jax.ShapeDtypeStruct((window, TILE), BF),
            jax.ShapeDtypeStruct((TILE, length), BF),
            jax.ShapeDtypeStruct((length, TILE), BF),
            number(tiles),
            number(tiles),
            number(tiles * window_tiles),
            number(tiles * window_tiles),
            number(1),
        ],
        name="setup",
    )(lengths, seq.reshape(1).astype(jnp.int32))


def own_kernel(place_ref, x_ref, wq_ref, wk_ref, wv_ref, vec_ref, q_ref, qt_ref, k_ref, kt_ref, v_ref, vt_ref, xt_ref):
    x = x_ref[...]
    q = ((dot(x, wq_ref[...]) + vec_ref[BIAS_Q : BIAS_Q + 1, :]) .astype(BF).astype(F32) * 0.125).astype(BF)
    q_ref[...] = q
    qt_ref[...] = q.T
    k = dot(x, wk_ref[...]).astype(BF)
    k_ref[...] = k
    kt_ref[...] = k.T
    v = (dot(x, wv_ref[...]) + vec_ref[BIAS_V : BIAS_V + 1, :]).astype(BF)
    v_ref[...] = v
    vt_ref[...] = v.T
    xt_ref[...] = x.T


def far_kernel(place_ref, x_ref, wk_ref, wv_ref, vec_ref, k_in, kt_in, v_in, vt_in, k_ref, kt_ref, v_ref, vt_ref):
    x = x_ref[...]
    k = dot(x, wk_ref[...]).astype(BF)
    k_ref[...] = k
    kt_ref[...] = k.T
    v = (dot(x, wv_ref[...]) + vec_ref[BIAS_V : BIAS_V + 1, :]).astype(BF)
    v_ref[...] = v
    vt_ref[...] = v.T


def project(x, x_far, wq, wk, wv, vectors, seq):
    length, features = x.shape
    far = x_far.shape[0]
    window = length + far
    rows = 256
    place = jnp.stack([seq * (far // rows), (1 - seq) * (length // rows)]).astype(jnp.int32)
    row = lambda i, place: (i, 0)
    col = lambda i, place: (0, i)
    whole = lambda i, place: (0, 0)
    once = pl.Buffered(1)
    weight = pl.BlockSpec((features, features), whole, pipeline_mode=once)
    vector = pl.BlockSpec(vectors.shape, whole, pipeline_mode=once)
    tall = jax.ShapeDtypeStruct((length, features), BF)
    flat = jax.ShapeDtypeStruct((features, length), BF)
    tall_window = jax.ShapeDtypeStruct((window, features), BF)
    flat_window = jax.ShapeDtypeStruct((features, window), BF)

    def window_blocks(which):
        down = pl.BlockSpec((rows, features), lambda i, place: (place[which] + i, 0))
        across = pl.BlockSpec((features, rows), lambda i, place: (0, place[which] + i))
        return [down, across, down, across]

    limit = pltpu.CompilerParams(vmem_limit_bytes=32 * VMEM_MIB)
    q, qt, k, kt, v, vt, xt = pl.pallas_call(
        own_kernel,
        grid_spec=pltpu.PrefetchScalarGridSpec(
            num_scalar_prefetch=1,
            grid=(length // rows,),
            in_specs=[pl.BlockSpec((rows, features), row), weight, weight, weight, vector],
            out_specs=[pl.BlockSpec((rows, features), row), pl.BlockSpec((features, rows), col)]
            + window_blocks(0)
            + [pl.BlockSpec((features, rows), col)],
        ),
        out_shape=[tall, flat, tall_window, flat_window, tall_window, flat_window, flat],
        compiler_params=limit,
        name="project_own",
    )(place, x, wq, wk, wv, vectors)
    anywhere = pl.BlockSpec(memory_space=pl.ANY)
    k, kt, v, vt = pl.pallas_call(
        far_kernel,
        grid_spec=pltpu.PrefetchScalarGridSpec(
            num_scalar_prefetch=1,
            grid=(far // rows,),
            in_specs=[pl.BlockSpec((rows, features), row), weight, weight, vector] + [anywhere] * 4,
            out_specs=window_blocks(1),
        ),
        out_shape=[tall_window, flat_window, tall_window, flat_window],
        input_output_aliases={5: 0, 6: 1, 7: 2, 8: 3},
        compiler_params=limit,
        name="project_far",
    )(place, x_far, wk, wv, vectors, k, kt, v, vt)
    return q, qt, k, kt, v, vt, xt


def loss_kernel(partners_ref, lengths_ref, place_ref, every_ref, pooled_ref, loss_ref, parts_ref):
    every = every_ref[...]
    count, features = every.shape
    own, _ = pooled_ref.shape
    first = place_ref[0] * own
    scores = 100.0 * dot(every, every, ((1,), (1,)))
    row = lax.broadcasted_iota(jnp.int32, (count, count), 0)
    lane = lax.broadcasted_iota(jnp.int32, (count, count), 1)
    scores = jnp.where(row == lane, BIG_NEG, scores)
    top = jnp.max(scores, 0, keepdims=True)
    log_sums = top + jnp.log(jnp.sum(jnp.exp(scores - top), 0, keepdims=True))
    mine = every_ref[pl.ds(pl.multiple_of(first, own), own), :]
    near = 100.0 * dot(mine, every, ((1,), (1,)))
    own_row = lax.broadcasted_iota(jnp.int32, (own, count), 0)
    own_lane = lax.broadcasted_iota(jnp.int32, (own, count), 1)
    near = jnp.where(own_row + first == own_lane, BIG_NEG, near)
    top = jnp.max(near, 1, keepdims=True)
    own_sums = top + jnp.log(jnp.sum(jnp.exp(near - top), 1, keepdims=True))
    target = jnp.concatenate(
        [jnp.where(own_lane[:1] == partners_ref[first + i], 1.0, 0.0) for i in range(own)], 0
    )
    picked = jnp.sum(jnp.where(target > 0.0, near, 0.0), 1, keepdims=True)
    loss_ref[...] = jnp.broadcast_to(own_sums - picked, loss_ref.shape)
    lane_row = own_lane[:1]

    def aim(n, held):
        return jnp.where(lane_row == n, partners_ref[n], held)

    aims = lax.fori_loop(0, count, aim, jnp.full((1, count), -1, jnp.int32))
    targeted = jnp.where(aims == own_row + first, 1.0, 0.0)
    both = jnp.exp(near - own_sums) - target + (jnp.exp(near - log_sums) - targeted)
    high, middle, low = split3(both)
    grad = 100.0 * (dot(high, every) + dot(middle, every) + dot(low, every))
    pooled = pooled_ref[...]
    inverse = lax.rsqrt(jnp.sum(pooled * pooled, 1, keepdims=True) + 1e-06)
    grad = inverse * grad - pooled * (inverse * inverse * inverse * jnp.sum(pooled * grad, 1, keepdims=True))
    sizes = jnp.concatenate(
        [jnp.full((1, features), lengths_ref[0, i].astype(F32), F32) for i in range(own)], 0
    )
    high, middle, low = split3(grad / sizes)
    parts_ref[...] = jnp.zeros(parts_ref.shape, BF)
    parts_ref[0:own, :] = high
    parts_ref[32 : 32 + own, :] = middle
    parts_ref[64 : 64 + own, :] = low


def contrast(partners, lengths, place, every, pooled):
    own, features = pooled.shape
    smem = pl.BlockSpec(memory_space=pltpu.SMEM)
    vmem = pl.BlockSpec(memory_space=pltpu.VMEM)
    return pl.pallas_call(
        loss_kernel,
        in_specs=[smem, smem, smem, vmem, vmem],
        out_specs=[vmem, vmem],
        out_shape=[jax.ShapeDtypeStruct((own, TILE), F32), jax.ShapeDtypeStruct((TILE, features), BF)],
        compiler_params=pltpu.CompilerParams(vmem_limit_bytes=48 * VMEM_MIB),
        name="contrast",
    )(partners, lengths, place.reshape(1).astype(jnp.int32), every, pooled)


def gelu_parts(u):
    size = jnp.abs(u)
    base = 1.0 + (0.3275911 * math.sqrt(0.5)) * size
    t = pl.reciprocal(base, approx=True)
    t = t * (2.0 - base * t)
    bell = jnp.exp(-0.5 * (u * u))
    poly = t * (0.127414796 + t * (-0.142248368 + t * (0.7107068705 + t * (-0.7265760135 + t * 0.5307027145))))
    tail = poly * bell
    below = jnp.where(u < 0.0, tail, 1.0 - tail)
    return u * below, below + u * bell * (1.0 / math.sqrt(2.0 * math.pi))


def normalized(resid):
    center = resid - jnp.mean(resid, -1, keepdims=True)
    scale = lax.rsqrt(jnp.mean(center * center, -1, keepdims=True) + EPS_NORM)
    return center * scale, scale


def feed_kernel(
    cb_ref, x_ref, member_ref, wo_ref, w1_ref, w2_ref, vec_ref,
    n1_ref, r1_ref, h_ref, f_ref, gp_ref, n2_ref, r2_ref, pool_ref,
):
    vector = lambda which: vec_ref[which : which + 1, :]
    attended = dot(cb_ref[...], wo_ref[...]) + vector(BIAS_O)
    unit, scale = normalized(x_ref[...].astype(F32) + attended)
    n1_ref[...] = unit.astype(BF)
    r1_ref[...] = scale
    hidden = unit * vector(GAIN_1) + vector(SHIFT_1)
    low = hidden.astype(BF)
    h_ref[...] = low.T
    resid = hidden + vector(BIAS_S)
    chunk = vec_ref.shape[1]
    for part in range(w1_ref.shape[1] // chunk):
        cols = slice(part * chunk, (part + 1) * chunk)
        u = dot(low, w1_ref[:, cols]) + vector(BIAS_E + part)
        active, slope = gelu_parts(u)
        active = active.astype(BF)
        f_ref[cols, :] = active.T
        gp_ref[:, cols] = slope.astype(BF)
        resid = resid + dot(active, w2_ref[cols, :])
    unit, scale = normalized(resid)
    n2_ref[...] = unit.astype(BF)
    r2_ref[...] = scale
    out = unit * vector(GAIN_2) + vector(SHIFT_2)
    high, middle, _ = split3(out)
    part = dot(member_ref[...], high) + dot(member_ref[...], middle)

    @pl.when(pl.program_id(0) == 0)
    def _():
        pool_ref[...] = part

    @pl.when(pl.program_id(0) > 0)
    def _():
        pool_ref[...] += part


def feed(cb, x, one_t, pass_count, wo, w1, w2, vectors):
    length, features = x.shape
    hidden = w1.shape[1]
    rows = 256
    row = lambda i: (i, 0)
    whole = lambda i: (0, 0)
    once = pl.Buffered(1)

    def full(array):
        return pl.BlockSpec(array.shape, whole, pipeline_mode=once)

    return pl.pallas_call(
        feed_kernel,
        grid=(length // rows,),
        in_specs=[
            pl.BlockSpec((rows, features), row),
            pl.BlockSpec((rows, features), row),
            pl.BlockSpec((pass_count, rows), lambda i: (0, i)),
        ]
        + [full(a) for a in (wo, w1, w2, vectors)],
        out_specs=[
            pl.BlockSpec((rows, features), row),
            pl.BlockSpec((rows, 1), row),
            pl.BlockSpec((features, rows), lambda i: (0, i)),
            pl.BlockSpec((hidden, rows), lambda i: (0, i)),
            pl.BlockSpec((rows, hidden), row),
            pl.BlockSpec((rows, features), row),
            pl.BlockSpec((rows, 1), row),
            pl.BlockSpec((pass_count, features), whole),
        ],
        out_shape=[
            jax.ShapeDtypeStruct((length, features), BF),
            jax.ShapeDtypeStruct((length, 1), F32),
            jax.ShapeDtypeStruct((features, length), BF),
            jax.ShapeDtypeStruct((hidden, length), BF),
            jax.ShapeDtypeStruct((length, hidden), BF),
            jax.ShapeDtypeStruct((length, features), BF),
            jax.ShapeDtypeStruct((length, 1), F32),
            jax.ShapeDtypeStruct((pass_count, features), F32),
        ],
        compiler_params=pltpu.CompilerParams(vmem_limit_bytes=60 * VMEM_MIB),
        name="feed",
    )(cb, x, one_t, wo, w1, w2, vectors)


def norm_back(grad, unit, scale, gain):
    wide = grad * gain
    return scale * (
        wide - jnp.mean(wide, -1, keepdims=True) - unit * jnp.mean(wide * unit, -1, keepdims=True)
    )


def add_rows(ref, row, value):
    ref[row : row + 1, :] += jnp.sum(value, 0, keepdims=True)


def start_back_kernel(spread_ref, pooled_ref, n2_ref, r2_ref, g2_ref, dr_ref, dy_ref, sums_ref):
    @pl.when(pl.program_id(0) == 0)
    def _():
        sums_ref[...] = jnp.zeros(sums_ref.shape, F32)

    grad = dot(spread_ref[...], pooled_ref[...])
    unit = n2_ref[...].astype(F32)
    add_rows(sums_ref, 0, grad * unit)
    add_rows(sums_ref, 1, grad)
    dr = norm_back(grad, unit, r2_ref[...], g2_ref[GAIN_2 : GAIN_2 + 1, :])
    dr_ref[...] = dr
    dy = dr.astype(BF)
    dy_ref[...] = dy
    add_rows(sums_ref, 2, dy.astype(F32))


def start_back(spread, pooled_parts, n2, r2, g2):
    length, features = n2.shape
    rows = 256
    row = lambda i: (i, 0)
    whole = lambda i: (0, 0)
    return pl.pallas_call(
        start_back_kernel,
        grid=(length // rows,),
        in_specs=[
            pl.BlockSpec((rows, spread.shape[1]), row),
            pl.BlockSpec(pooled_parts.shape, whole),
            pl.BlockSpec((rows, features), row),
            pl.BlockSpec((rows, 1), row),
            pl.BlockSpec(g2.shape, whole),
        ],
        out_specs=[
            pl.BlockSpec((rows, features), row),
            pl.BlockSpec((rows, features), row),
            pl.BlockSpec((8, features), whole),
        ],
        out_shape=[
            jax.ShapeDtypeStruct((length, features), F32),
            jax.ShapeDtypeStruct((length, features), BF),
            jax.ShapeDtypeStruct((8, features), F32),
        ],
        name="start_back",
    )(spread, pooled_parts, n2, r2, g2)


def expand_back_kernel(dy_ref, gp_ref, w2_ref, du_ref, wide_sums_ref):
    @pl.when(pl.program_id(0) == 0)
    def _():
        wide_sums_ref[...] = jnp.zeros(wide_sums_ref.shape, F32)

    dy = dy_ref[...]
    chunk = 512
    for start in range(0, w2_ref.shape[0], chunk):
        cols = slice(start, start + chunk)
        slope = gp_ref[:, cols].astype(F32)
        du = (slope * dot(dy, w2_ref[cols, :], ((1,), (1,)))).astype(BF)
        du_ref[:, cols] = du
        wide_sums_ref[0:1, cols] += jnp.sum(du.astype(F32), 0, keepdims=True)


def expand_back(dy, gp, w2):
    length, features = dy.shape
    hidden = gp.shape[1]
    rows = 256
    row = lambda i: (i, 0)
    whole = lambda i: (0, 0)
    return pl.pallas_call(
        expand_back_kernel,
        grid=(length // rows,),
        in_specs=[
            pl.BlockSpec((rows, features), row),
            pl.BlockSpec((rows, hidden), row),
            pl.BlockSpec(w2.shape, whole, pipeline_mode=pl.Buffered(1)),
        ],
        out_specs=[pl.BlockSpec((rows, hidden), row), pl.BlockSpec((8, hidden), whole)],
        out_shape=[jax.ShapeDtypeStruct((length, hidden), BF), jax.ShapeDtypeStruct((8, hidden), F32)],
        compiler_params=pltpu.CompilerParams(vmem_limit_bytes=60 * VMEM_MIB),
        name="expand_back",
    )(dy, gp, w2)


def hidden_back_kernel(dr2_ref, du_ref, n1_ref, r1_ref, w1_ref, wo_ref, g1_ref, ct_ref, dr1_ref, da_ref, dc_ref, dct_ref, delta_ref, sums_ref):
    @pl.when(pl.program_id(0) == 0)
    def _():
        sums_ref[...] = jnp.zeros(sums_ref.shape, F32)

    dh = dr2_ref[...] + dot(du_ref[...], w1_ref[...], ((1,), (1,)))
    unit = n1_ref[...].astype(F32)
    add_rows(sums_ref, 0, dh * unit)
    add_rows(sums_ref, 1, dh)
    dr = norm_back(dh, unit, r1_ref[...], g1_ref[GAIN_1 : GAIN_1 + 1, :])
    dr1_ref[...] = dr
    da = dr.astype(BF)
    da_ref[...] = da
    add_rows(sums_ref, 2, da.astype(F32))
    dc_ref[...] = dot(da, wo_ref[...], ((1,), (1,))).astype(BF)
    dct = dot(wo_ref[...], da, ((1,), (1,))).astype(BF)
    dct_ref[...] = dct
    product = dct.astype(F32) * ct_ref[...]
    size = product.shape[0] // HEADS
    delta_ref[...] = jnp.concatenate(
        [jnp.sum(product[head * size : (head + 1) * size], 0, keepdims=True) for head in range(HEADS)], 0
    )


def hidden_back(dr2, du, n1, r1, w1, wo, g1, ct):
    length, features = dr2.shape
    hidden = du.shape[1]
    rows = 256
    row = lambda i: (i, 0)
    whole = lambda i: (0, 0)
    once = pl.Buffered(1)

    def full(array):
        return pl.BlockSpec(array.shape, whole, pipeline_mode=once)

    return pl.pallas_call(
        hidden_back_kernel,
        grid=(length // rows,),
        in_specs=[
            pl.BlockSpec((rows, features), row),
            pl.BlockSpec((rows, hidden), row),
            pl.BlockSpec((rows, features), row),
            pl.BlockSpec((rows, 1), row),
            full(w1),
            full(wo),
            full(g1),
            pl.BlockSpec((features, rows), lambda i: (0, i)),
        ],
        out_specs=[
            pl.BlockSpec((rows, features), row),
            pl.BlockSpec((rows, features), row),
            pl.BlockSpec((rows, features), row),
            pl.BlockSpec((features, rows), lambda i: (0, i)),
            pl.BlockSpec((HEADS, rows), lambda i: (0, i)),
            pl.BlockSpec((8, features), whole),
        ],
        out_shape=[
            jax.ShapeDtypeStruct((length, features), F32),
            jax.ShapeDtypeStruct((length, features), BF),
            jax.ShapeDtypeStruct((length, features), BF),
            jax.ShapeDtypeStruct((features, length), BF),
            jax.ShapeDtypeStruct((HEADS, length), F32),
            jax.ShapeDtypeStruct((8, features), F32),
        ],
        compiler_params=pltpu.CompilerParams(vmem_limit_bytes=60 * VMEM_MIB),
        name="hidden_back",
    )(dr2, du, n1, r1, w1, wo, g1, ct)


def swap_seq(array):
    return lax.ppermute(array, "seq", [(0, 1), (1, 0)])


def swap_dp(array, bit):
    count = lax.axis_size("dp")
    return lax.ppermute(array, "dp", [(i, i ^ (1 << bit)) for i in range(count)])


def swap_crossed(array, bits):
    count = lax.axis_size("dp")
    pairs = [(2 * i + s, 2 * (i ^ (1 << bits[s])) + s) for i in range(count) for s in range(2)]
    return lax.ppermute(array, ("dp", "seq"), pairs)


def pick_half(array, axis, which):
    half = array.shape[axis] // 2
    return lax.dynamic_slice_in_dim(array, which * half, half, axis)


def join(mine, other, axis, place):
    return jnp.where(
        place == 0, jnp.concatenate([mine, other], axis), jnp.concatenate([other, mine], axis)
    )


def halving_axis(shape):
    rows, cols = shape
    if rows % 32 == 0:
        return 0
    if cols % 256 == 0:
        return 1
    return 0


COLS = 384


def partial_kernel(counts, add, place_ref, *refs):
    sources = len(counts)
    lefts, rights = refs[:sources], refs[sources : 2 * sources]
    out_ref = refs[-1]
    block = place_ref[0] * (sum(counts) // 2) + pl.program_id(1)
    start = 0
    for left, right, count in zip(lefts, rights, counts):

        @pl.when((block >= start) & (block < start + count))
        def _(left=left, right=right):
            value = dot(left[...], right[...])
            if add:
                value = value + refs[2 * sources][...].astype(F32)
            out_ref[...] = value.astype(BF)

        start += count


def partial_grads(sources, half, part, parts, received=None):
    counts = [right.shape[1] // COLS for _, right in sources]
    total = sum(counts) // 2
    length = sources[0][0].shape[1]
    rows = sources[0][0].shape[0] // parts
    step = min(rows, 768)
    blocks = rows // step
    starts = [sum(counts[:i]) for i in range(len(counts))]
    in_specs = [
        pl.BlockSpec((step, length), lambda i, j, place: (place[1] * blocks + i, 0)) for _ in sources
    ]
    for start, count in zip(starts, counts):
        in_specs.append(
            pl.BlockSpec(
                (length, COLS),
                lambda i, j, place, start=start, count=count: (
                    0,
                    jnp.clip(place[0] * total + j - start, 0, count - 1),
                ),
            )
        )
    operands = [left for left, _ in sources] + [right for _, right in sources]
    if received is not None:
        in_specs.append(pl.BlockSpec((step, COLS), lambda i, j, place: (place[1] * blocks + i, j)))
        operands.append(received)
    return pl.pallas_call(
        functools.partial(partial_kernel, counts, received is not None),
        grid_spec=pltpu.PrefetchScalarGridSpec(
            num_scalar_prefetch=1,
            grid=(blocks, total),
            in_specs=in_specs,
            out_specs=pl.BlockSpec((step, COLS), lambda i, j, place: (i, j)),
        ),
        out_shape=jax.ShapeDtypeStruct((rows, total * COLS), BF),
        compiler_params=pltpu.CompilerParams(vmem_limit_bytes=60 * VMEM_MIB),
        name="partial_grads",
    )(jnp.stack([half, part]).astype(jnp.int32), *operands)


def fold_kernel(parts, place_ref, keep_ref, other_ref, *out_refs):
    total = (keep_ref[...].astype(F32) + other_ref[...].astype(F32)).astype(BF)
    for m in range(parts):

        @pl.when(pl.program_id(0) == m)
        def _(m=m):
            out_refs[m][...] = total


def fold(keep, other, place, parts):
    rows, cols = keep.shape[0] // parts, keep.shape[1]
    picked = pl.BlockSpec((rows, cols), lambda m, place: (place[0] ^ m, 0))
    return pl.pallas_call(
        functools.partial(fold_kernel, parts),
        grid_spec=pltpu.PrefetchScalarGridSpec(
            num_scalar_prefetch=1,
            grid=(parts,),
            in_specs=[picked, picked],
            out_specs=[pl.BlockSpec((rows, cols), lambda m, place: (0, 0))] * parts,
        ),
        out_shape=[jax.ShapeDtypeStruct((rows, cols), BF)] * parts,
        compiler_params=pltpu.CompilerParams(vmem_limit_bytes=60 * VMEM_MIB),
        name="fold",
    )(place.reshape(1).astype(jnp.int32), keep, other)


def assemble_kernel(counts, place_ref, own_ref, other_ref, *out_refs):
    block = pl.program_id(0)
    per_half = sum(counts) // 2
    mine = block // per_half == place_ref[0]
    shards, rows = own_ref.shape[0], own_ref.shape[1]

    def write(source, offset):
        start = 0
        for out_ref, count in zip(out_refs, counts):

            @pl.when((block >= start) & (block < start + count))
            def _(out_ref=out_ref):
                for shard in range(shards):
                    out_ref[shard * rows : (shard + 1) * rows, :] = source[shard ^ offset].astype(F32)

            start += count

    @pl.when(mine)
    def _():
        write(own_ref, place_ref[1])

    @pl.when(jnp.logical_not(mine))
    def _():
        write(other_ref, place_ref[2])


def assemble(own, other, places, counts):
    shards, rows, _ = own.shape
    per_half = sum(counts) // 2
    out_specs, start = [], 0
    for count in counts:
        out_specs.append(
            pl.BlockSpec(
                (shards * rows, COLS), lambda g, place, start=start, count=count: (0, jnp.clip(g - start, 0, count - 1))
            )
        )
        start += count

    def shard_block(flag):
        return pl.BlockSpec(
            (shards, rows, COLS),
            lambda g, place: (0, 0, jnp.where((g // per_half == place[0]) == flag, g % per_half, 0)),
        )

    return pl.pallas_call(
        functools.partial(assemble_kernel, counts),
        grid_spec=pltpu.PrefetchScalarGridSpec(
            num_scalar_prefetch=1,
            grid=(2 * per_half,),
            in_specs=[shard_block(True), shard_block(False)],
            out_specs=out_specs,
        ),
        out_shape=[jax.ShapeDtypeStruct((shards * rows, count * COLS), F32) for count in counts],
        compiler_params=pltpu.CompilerParams(vmem_limit_bytes=60 * VMEM_MIB),
        name="assemble",
    )(jnp.stack(places).astype(jnp.int32), own, other)


class GradTotal:
    steps = 8

    def __init__(self, sources):
        self.sources, self.step = sources, 0
        seq, dp = lax.axis_index("seq"), lax.axis_index("dp")
        self.seq, self.far = seq, (dp >> 2) & 3
        self.near = ((dp >> seq) & 1, (dp >> (1 - seq)) & 1)
        self.state = None

    def offset(self, seq):
        dp = lax.axis_index("dp")
        return ((dp >> seq) & 1) * 8 + ((dp >> (1 - seq)) & 1) * 4 + ((dp >> 2) & 3)

    def prepare(self):
        step = self.step
        if step == 0:
            self.out = [partial_grads(self.sources, 1 - self.seq, jnp.int32(0), 1)]
        elif step == 1:
            self.out = [partial_grads(self.sources, self.seq, 1 - self.near[0], 2, self.got[0])]
            self.swapped = self.got[0]
        elif step == 2:
            keep = partial_grads(self.sources, self.seq, self.near[0], 2, self.swapped)
            self.keep, send = fold(keep, self.got[0], self.near[1], 2)
            self.out = [send]
        elif step == 3:
            self.keep, *self.out = fold(self.keep, self.got[0], self.far, 4)
        elif step == 4:
            total = self.keep.astype(F32)
            for other in self.got:
                total = total + other.astype(F32)
            self.out = [total.astype(BF)]
        elif step == 5:
            self.out = [jnp.stack(self.out + self.got)]
        else:
            self.out = [jnp.concatenate(self.out + self.got)]

    def exchange(self):
        step, count = self.step, lax.axis_size("dp")
        if step in (0, 7):
            self.got = [swap_seq(self.out[0])]
        elif step in (1, 6):
            self.got = [swap_crossed(self.out[0], (0, 1))]
        elif step in (2, 5):
            self.got = [swap_crossed(self.out[0], (1, 0))]
        else:
            sends = self.out if step == 3 else self.out * 3
            self.got = [
                lax.ppermute(send, "dp", [(i, i ^ (m << 2)) for i in range(count)])
                for m, send in zip((1, 2, 3), sends)
            ]
        self.step += 1

    def done(self):
        return self.step == self.steps

    def whole(self, counts):
        places = [self.seq, self.offset(self.seq), self.offset(1 - self.seq)]
        return assemble(self.out[0], self.got[0], places, counts)


def plain_total(partial):
    seq, index = lax.axis_index("seq"), lax.axis_index("dp")
    block = (pick_half(partial, 0, seq).astype(F32) + swap_seq(pick_half(partial, 0, 1 - seq)).astype(F32)).astype(BF)
    steps = []
    for bit in range(int(math.log2(lax.axis_size("dp")))):
        place, axis = (index >> bit) & 1, halving_axis(block.shape)
        steps.append((bit, place, axis))
        other = swap_dp(pick_half(block, axis, 1 - place), bit)
        block = (pick_half(block, axis, place).astype(F32) + other.astype(F32)).astype(BF)
    for bit, place, axis in reversed(steps):
        block = join(block, swap_dp(block, bit), axis, place)
    return join(block, swap_seq(block), 0, seq).astype(F32)


class PlainTotal:
    def __init__(self, sources):
        self.sources = sources

    def done(self):
        return True

    def whole(self, counts):
        return [plain_total(dot(left, right).astype(BF)) for left, right in self.sources]


class Small:
    def __init__(self, partial):
        self.block, self.step = partial, 0
        self.steps = 1 + int(math.log2(lax.axis_size("dp")))

    def prepare(self):
        if self.step:
            self.block = self.block + self.got[0]
        self.out = [self.block]

    def exchange(self):
        block = self.out[0]
        self.block = block
        self.got = [swap_seq(block) if self.step == 0 else swap_dp(block, self.step - 1)]
        self.step += 1

    def done(self):
        return self.step == self.steps

    def whole(self):
        return self.block + self.got[0]


def fence(*values):
    return lax.optimization_barrier(values)


def beside(sums, work, *inputs):
    live = [total for total in sums if not total.done()]
    for total in live:
        total.prepare()
    inputs, sends = fence(inputs, [total.out for total in live])
    for total, send in zip(live, sends):
        total.out = send
        total.exchange()
    result, received = fence(work(*inputs), [total.got for total in live])
    for total, got in zip(live, received):
        total.got = got
    return result


def body(
    tokens, lengths, partners, query_proj, query_bias, key_proj, value_proj, value_bias, output_proj, output_bias,
    first_gain, first_shift, expand_proj, expand_bias, shrink_proj, shrink_bias, second_gain, second_shift,
):
    _, length, features = tokens.shape
    pass_count = lengths.shape[1]
    seq = lax.axis_index("seq")
    dp = lax.axis_index("dp")
    far = length // 2
    window = length + far
    x = tokens[0]

    x_far = swap_seq(lax.dynamic_slice_in_dim(x, (1 - seq) * far, far, 0))
    vectors = jnp.concatenate(
        [
            jnp.stack(
                [
                    output_bias, first_gain, first_shift, shrink_bias, second_gain, second_shift, query_bias, value_bias,
                ]
            ),
            expand_bias.reshape(-1, features),
        ]
    )
    aux, one_t, spread, key_lo, key_hi, *pair_list = setup(lengths, seq, length, window)
    queries, queries_t, keys, keys_t, values, values_t, x_t = project(
        x, x_far, query_proj, key_proj, value_proj, vectors, seq
    )
    context_low, context_t, context_low_t, lse = attend(queries_t, one_t, keys, values_t, aux, key_lo, key_hi)
    unit1, scale1, hidden_t, active_t, slope, unit2, scale2, pooled_part = feed(
        context_low, x, one_t, pass_count, output_proj, expand_proj, shrink_proj, vectors
    )

    lengths_wide = lengths.reshape(pass_count, 1).astype(F32)
    pooled = (pooled_part + swap_seq(pooled_part)) / lengths_wide
    inverse = lax.rsqrt(jnp.sum(pooled * pooled, -1, keepdims=True) + 1e-06)
    every = (pooled * inverse).astype(BF)
    for bit in range(int(math.log2(lax.axis_size("dp")))):
        every = join(every, swap_dp(every, bit), 0, (dp >> bit) & 1)
    passage_loss, pooled_parts = contrast(partners, lengths, dp, every, pooled)
    passage_loss = passage_loss[:, 0]

    grad_second, grad_shrunk, sums2 = start_back(spread, pooled_parts, unit2, scale2, vectors)
    Sum = GradTotal if lax.axis_size("dp") == 16 else PlainTotal
    shrink_sum = Sum([(active_t, grad_shrunk)])
    grad_expanded, wide_sums = beside([shrink_sum], expand_back, grad_shrunk, slope, shrink_proj)
    grad_first, grad_attended, grad_context, grad_context_t, delta, sums1 = beside(
        [shrink_sum],
        lambda second, expanded: hidden_back(
            second, expanded, unit1, scale1, expand_proj, output_proj, vectors, context_t
        ),
        grad_second,
        grad_expanded,
    )
    expand_sum = Sum([(hidden_t, grad_expanded), (context_low_t, grad_attended)])
    parts = 2
    pieces = []
    for part in range(parts):

        def attention_work(grad_context):
            return attend_back(
                part, parts, pair_list, queries, queries_t, grad_context, grad_context_t, one_t, lse, delta, keys,
                keys_t, values, aux,
            )

        pieces.append(beside([shrink_sum, expand_sum], attention_work, grad_context))
    grad_query, grad_keys, grad_values = (jnp.concatenate(piece, 1) for piece in zip(*pieces))

    def gather_far(window_grad):
        own = lax.dynamic_slice_in_dim(window_grad, seq * far, length, 0)
        other = swap_seq(lax.dynamic_slice_in_dim(window_grad, (1 - seq) * length, far, 0))
        nothing = jnp.zeros((far, features), BF)
        return (own.astype(F32) + join(other, nothing, 0, 1 - seq).astype(F32)).astype(BF)

    def last_work(grad_keys, grad_values):
        return gather_far(grad_keys), gather_far(grad_values)

    keys_grad, values_grad = beside([shrink_sum, expand_sum], last_work, grad_keys, grad_values)
    attention_sum = Sum([(x_t, grad_query), (x_t, keys_grad), (x_t, values_grad)])

    def tokens_work(grad_first, grad_query, keys_grad, values_grad):
        tokens_grad = (
            grad_first
            + dot(grad_query, query_proj, ((1,), (1,)))
            + dot(keys_grad, key_proj, ((1,), (1,)))
            + dot(values_grad, value_proj, ((1,), (1,)))
        )[None]
        small = jnp.concatenate(
            [
                sums2[:3],
                sums1[:3],
                jnp.sum(grad_query.astype(F32), 0, keepdims=True),
                jnp.sum(values_grad.astype(F32), 0, keepdims=True),
                wide_sums[:1].reshape(-1, features),
            ],
            0,
        )
        return tokens_grad, small

    tokens_grad, small = beside(
        [shrink_sum, expand_sum, attention_sum], tokens_work, grad_first, grad_query, keys_grad, values_grad
    )
    small_sum = Small(small)
    sums = [shrink_sum, expand_sum, attention_sum, small_sum]
    blocks = {shrink_sum: [features // COLS], expand_sum: [expand_proj.shape[1] // COLS, features // COLS]}
    wholes = {}
    while not all(total.done() for total in sums):
        ready = [total for total in (shrink_sum, expand_sum) if total.done() and total not in wholes][:1]
        results = beside(sums, lambda _: [total.whole(blocks[total]) for total in ready], small)
        wholes.update(zip(ready, results))
    for total in (shrink_sum, expand_sum):
        if total not in wholes:
            wholes[total] = total.whole(blocks[total])
    small = small_sum.whole()
    (shrink_total,) = wholes[shrink_sum]
    expand_total, output_total = wholes[expand_sum]
    query_total, key_total, value_total = attention_sum.whole([features // COLS] * 3)
    return (
        passage_loss,
        tokens_grad,
        query_total,
        small[6],
        key_total,
        value_total,
        small[7],
        output_total,
        small[5],
        small[3],
        small[4],
        expand_total,
        small[8:].reshape(-1),
        shrink_total,
        small[2],
        small[0],
        small[1],
    )


def solution(mesh):
    placed = (P("dp", "seq", None), P("dp", None)) + (P(),) * 16
    return jax.shard_map(
        body,
        mesh=mesh,
        in_specs=placed,
        out_specs=(P("dp"), P("dp", "seq", None)) + (P(),) * 15,
        check_vma=False,
    )
```

time: 588 us -> 473 us (0.80)
  Pallas kernels: 136 us -> 262 us
  waiting for transfers between devices: 161 us -> 71.7 us
  other arithmetic: 83.2 us -> 21.1 us
  matrix products: 46.2 us -> 6.05 us
  starting transfers between devices: 104 us -> 71.4 us
  local copies, waits for them, and re-layouts: 47.3 us -> 30.1 us
    ppermute x88 -> x8, waiting for transfers between devices: 160 us -> 24 us  [swap_dp(): return lax.ppermute(array, 'dp', [(i, i ^ 1 << bit) for i in range(count)])]
    pallas_call x1 -> x24, Pallas kernels: 23.4 us -> 157 us  [the longest x9 65.2 us: partial_grads(): pl.pallas_call(functools.partial(partial_kernel, counts, received is not...]
    ppermute x88 -> x8, starting transfers between devices: 87.6 us -> 12.7 us  [swap_dp(): return lax.ppermute(array, 'dp', [(i, i ^ 1 << bit) for i in range(count)])]
    convert_element_type x55 -> x5, other arithmetic: 59.1 us -> 6.38 us  [the longest x2 6.14 us: gather_far(): (own.astype(F32) + join(other, nothing, 0, 1 - seq).astype(F32)).astype(BF)]
    ppermute x0 -> x30, waiting for transfers between devices: none -> 44.8 us  [the longest x12 27.7 us: swap_crossed(): return lax.ppermute(array, ('dp', 'seq'), pairs)]
    ppermute x0 -> x30, starting transfers between devices: none -> 41.8 us  [the longest x18 29.8 us: exchange(): lax.ppermute(send, 'dp', [(i, i ^ m << 2) for i in range(count)])]
    dot_general x13 -> x3, matrix products: 44.5 us -> 6.05 us  [dot(): lax.dot_general(left, right, (over, ((), ())), preferred_element_type=F32)]
    select_n x43 -> x4, other arithmetic: 10.9 us -> 0.14 us  [join(): jnp.where(place == 0, jnp.concatenate([mine, other], axis), jnp.concatena...]
  transfers between devices with their start and end apart: 105 -> 49, of which waited for: 55 -> 16; matrix products, arithmetic and copies ran while one was open for 21% -> 5% of each run, Pallas kernels for 9% -> 27%
where the time goes in v2:
time: 473 us; the launch traced here: 464 us
  Pallas kernels  262 us (55%)
  waiting for transfers between devices  71.7 us (15%)
  starting transfers between devices  71.4 us (15%)
  local copies, waits for them, and re-layouts  30.1 us (6%)
  other arithmetic  21.1 us (4%)
  matrix products  6.05 us (1%)
    pallas_call x9, Pallas kernels, partial_grads(): pl.pallas_call(functools.partial(partial_kernel, counts, received is not...  65.2 us
    pallas_call x2, Pallas kernels, attend_back(): pl.pallas_call(attend_back_kernel, grid_spec=pltpu.PrefetchScalarGridSpec...  48 us
    pallas_call x1, Pallas kernels, feed(): pl.pallas_call(feed_kernel, grid=(length // rows,), in_specs=[pl.BlockSpe...  31 us
    ppermute x18, starting transfers between devices, exchange(): lax.ppermute(send, 'dp', [(i, i ^ m << 2) for i in range(count)])  29.8 us
    ppermute x12, waiting for transfers between devices, swap_crossed(): return lax.ppermute(array, ('dp', 'seq'), pairs)  27.7 us
    pallas_call x3, Pallas kernels, assemble(): pl.pallas_call(functools.partial(assemble_kernel, counts), grid_spec=pltp...  25.6 us
    ppermute x8, waiting for transfers between devices, swap_dp(): return lax.ppermute(array, 'dp', [(i, i ^ 1 << bit) for i in range(count)])  24 us
    pallas_call x1, Pallas kernels, attend(): pl.pallas_call(attend_kernel, grid_spec=pltpu.PrefetchScalarGridSpec(num_...  20 us
  transfers between devices with their start and end apart: 49, of which 16 were waited for; matrix products, arithmetic and copies ran while one was open for 5% of the time, Pallas kernels for 27%

profile of v2, /device:TPU:0, one launch (start us, length us, event | category | flops | bytes accessed | tf_op | source)
XLA Modules:
  0.0 463.7 jit_solution(4986557076108607420)
XLA Ops:
  3.6 5.1 %setup.1 = (bf16[1536,128]{1,0:T(8,128)(2,1)}, bf16[128,1024]{1,0:T(8,128)(2,1)}, bf16[1024,128]{1,0:T(8,128)(2,1)}, s32[8]{0:T(128)}, s32[8]{0:T(128)}, /*index=5*/s32[96]{0:T(128)}, s32[96]{0:T(128)}, s32[1]{0:T(128)}) custom-call(s32[1,16]{1,0:T(1,128)} %lengths_ref.3, s32[1]{0:T(128)} %bitcast.1.seq_ref), custom_call_target="tpu_custom_call" | custom-call | tf_op jit(solution)/shard_map/setup/pallas_call | solution.py:334
  15.3 6.1 %project_own.1 = (bf16[1024,768]{1,0:T(8,128)(2,1)S(1)}, bf16[768,1024]{1,0:T(8,128)(2,1)S(1)}, bf16[1536,768]{1,0:T(8,128)(2,1)S(1)}, bf16[768,1536]{1,0:T(8,12...) custom-call(s32[2]{0:T(128)S(1)} %get-tuple-element.389.place_ref, ...), custom_call_target="tpu_custom_call" | custom-call | tf_op jit(solution)/shard_map/project_own/pallas_call | solution.py:399
  30.7 20.0 %attend.1 = (bf16[1024,768]{1,0:T(8,128)(2,1)}, f32[768,1024]{1,0:T(8,128)}, bf16[768,1024]{1,0:T(8,128)(2,1)}, f32[12,1024]{1,0:T(8,128)}) custom-call(s32[8]{0:T(128)} %get-tuple-element.198.lo_ref, s32[8]{0:T(128)} %get-tuple-element.199.hi_ref, bf16[768,1024]{1,0:T(8,128)(2,1)} %copy-done.4, bf16[128,1024]{1,0:T(8,128)(2,1)} %get-tuple-element.201.onet_ref.member_ref, ...), custom_call_target="tpu_custom_call" | custom-call | tf_op jit(solution)/shard_map/attend/pallas_call | solution.py:125
  50.7 31.0 %feed.1 = (bf16[1024,768]{1,0:T(8,128)(2,1)}, f32[1024,1]{1,0:T(8,128)}, bf16[768,1024]{1,0:T(8,128)(2,1)}, bf16[3072,1024]{1,0:T(8,128)(2,1)}, bf16[1024,3072]{...) custom-call(bf16[1024,768]{1,0:T(8,128)(2,1)} %get-tuple-element.209.cb_ref, ...), custom_call_target="tpu_custom_call" | custom-call | tf_op jit(solution)/shard_map/feed/pallas_call | solution.py:557
  92.3 3.8 collective-permute-start.3
  98.3 4.6 collective-permute-done.4
  103.9 7.9 %collective-permute-done.5 = bf16[128,768]{1,0:T(8,128)(2,1)S(1)} collective-permute-done((bf16[128,768]{1,0:T(8,128)(2,1)S(1)}, bf16[128,768]{1,0:T(8,128)(2,1)S(1)}, u32[]{:S(2)}, u32[]{:S(2)}) %collective-permute-start.5) | collective-permute-done | bytes 196640 | tf_op jit(solution)/shard_map/ppermute | solution.py:758
  115.6 5.6 %start_back.1 = (f32[1024,768]{1,0:T(8,128)}, bf16[1024,768]{1,0:T(8,128)(2,1)}, f32[8,768]{1,0:T(8,128)}) custom-call(bf16[1024,128]{1,0:T(8,128)(2,1)} %get-tuple-element.212.spread_ref, bf16[128,768]{1,0:T(8,128)(2,1)} %copy-done.14, bf16[1024,768]{1,0:T(8,128)(2,1)} %get-tuple-element.214.n2_ref, f32[1024,1]{1,0:T(8,128)} %get-tuple-element.215.r2_ref, ...), custom_call_target="tpu_custom_call" | custom-call | tf_op jit(solution)/shard_map/start_back/pallas_call | solution.py:623
  121.2 7.8 %partial_grads.9 = bf16[3072,384]{1,0:T(8,128)(2,1)} custom-call(s32[2]{0:T(128)} %get-tuple-element.390.place_ref, bf16[3072,1024]{1,0:T(8,128)(2,1)} %get-tuple-element.219.refs_0_, bf16[1024,768]{1,0:T(8,128)(2,1)} %get-tuple-element.220.refs_1_.dy_ref), custom_call_target="tpu_custom_call" | custom-call | tf_op jit(solution)/shard_map/partial_grads/pallas_call | solution.py:833
  129.7 11.4 %expand_back.1 = (bf16[1024,3072]{1,0:T(8,128)(2,1)}, f32[8,3072]{1,0:T(8,128)}) custom-call(bf16[1024,768]{1,0:T(8,128)(2,1)} %get-tuple-element.220.refs_1_.dy_ref, bf16[1024,3072]{1,0:T(8,128)(2,1)} %get-tuple-element.221.gp_ref, bf16[3072,768]{1,0:T(8,128)(2,1)} %w2_ref.2), custom_call_target="tpu_custom_call" | custom-call | tf_op jit(solution)/shard_map/expand_back/pallas_call | solution.py:668
  141.1 5.3 %partial_grads.10 = bf16[1536,384]{1,0:T(8,128)(2,1)} custom-call(s32[2]{0:T(128)} %pad_add_fusion.2.place_ref, bf16[3072,1024]{1,0:T(8,128)(2,1)} %get-tuple-element.219.refs_0_, bf16[1024,768]{1,0:T(8,128)(2,1)} %get-tuple-element.220.refs_1_.dy_ref, bf16[3072,384]{1,0:T(8,128)(2,1)} %collective-permute-done.6.refs_2_), custom_call_target="tpu_custom_call" | custom-call | tf_op jit(solution)/shard_map/partial_grads/pallas_call | solution.py:833
  147.5 5.3 %partial_grads.11.keep_ref = bf16[1536,384]{1,0:T(8,128)(2,1)} custom-call(s32[2]{0:T(128)} %pad_add_fusion.3.place_ref, bf16[3072,1024]{1,0:T(8,128)(2,1)} %get-tuple-element.219.refs_0_, bf16[1024,768]{1,0:T(8,128)(2,1)} %get-tuple-element.220.refs_1_.dy_ref, bf16[3072,384]{1,0:T(8,128)(2,1)} %collective-permute-done.6.refs_2_), custom_call_target="tpu_custom_call" | custom-call | tf_op jit(solution)/shard_map/partial_grads/pallas_call | solution.py:833
  152.9 17.8 %hidden_back.1 = (f32[1024,768]{1,0:T(8,128)}, bf16[1024,768]{1,0:T(8,128)(2,1)}, bf16[1024,768]{1,0:T(8,128)(2,1)}, bf16[768,1024]{1,0:T(8,128)(2,1)}, f32[12,1024]{1,0:T(8,128)}, /*index=5*/f32[8,768]{1,0:T(8,128)}) custom-call(f32[1024,768]{1,0:T(8,128)} %get-tuple-element.228.dr2_ref, bf16[1024,3072]{1,0:T(8,128)(2,1)} %get-tuple-element.229.du_ref.refs_2_, ...), custom_call_target="tpu_custom_call" | custom-call | tf_op jit(solution)/shard_map/hidden_back/pallas_call | solution.py:718
  174.6 9.7 %partial_grads.12 = bf16[768,1920]{1,0:T(8,128)(2,1)} custom-call(s32[2]{0:T(128)} %get-tuple-element.390.place_ref, bf16[768,1024]{1,0:T(8,128)(2,1)} %get-tuple-element.248.refs_0_, bf16[768,1024]{1,0:T(8,128)(2,1)} %get-tuple-element.249.refs_1_, bf16[1024,3072]{1,0:T(8,128)(2,1)} %get-tuple-element.229.du_ref.refs_2_, ...), custom_call_target="tpu_custom_call" | custom-call | tf_op jit(solution)/shard_map/partial_grads/pallas_call | solution.py:833
  187.4 24.0 %attend_back.2 = (bf16[1024,384]{1,0:T(8,128)(2,1)}, bf16[1536,384]{1,0:T(8,128)(2,1)}, bf16[1536,384]{1,0:T(8,128)(2,1)}) custom-call(s32[96]{0:T(128)} %get-tuple-element.241.kt_ref, s32[96]{0:T(128)} %get-tuple-element.242.qt_list_ref, s32[1]{0:T(128)} %get-tuple-element.243.count_ref, bf16[1024,768]{1,0:T(8,128)(2,1)} %copy-done.8, ...), custom_call_target="tpu_custom_call" | custom-call | tf_op jit(solution)/shard_map/attend_back/pallas_call | solution.py:219
  211.4 7.8 %partial_grads.13 = bf16[384,1920]{1,0:T(8,128)(2,1)} custom-call(s32[2]{0:T(128)} %pad_add_fusion.2.place_ref, bf16[768,1024]{1,0:T(8,128)(2,1)} %get-tuple-element.248.refs_0_, bf16[768,1024]{1,0:T(8,128)(2,1)} %get-tuple-element.249.refs_1_, bf16[1024,3072]{1,0:T(8,128)(2,1)} %get-tuple-element.229.du_ref.refs_2_, ...), custom_call_target="tpu_custom_call" | custom-call | tf_op jit(solution)/shard_map/partial_grads/pallas_call | solution.py:833
  224.0 4.6 collective-permute-start.11
  228.6 7.8 %partial_grads.14.keep_ref = bf16[384,1920]{1,0:T(8,128)(2,1)} custom-call(s32[2]{0:T(128)} %pad_add_fusion.3.place_ref, bf16[768,1024]{1,0:T(8,128)(2,1)} %get-tuple-element.248.refs_0_, bf16[768,1024]{1,0:T(8,128)(2,1)} %get-tuple-element.249.refs_1_, bf16[1024,3072]{1,0:T(8,128)(2,1)} %get-tuple-element.229.du_ref.refs_2_, ...), custom_call_target="tpu_custom_call" | custom-call | tf_op jit(solution)/shard_map/partial_grads/pallas_call | solution.py:833
  236.4 24.0 %attend_back.3 = (bf16[1024,384]{1,0:T(8,128)(2,1)}, bf16[1536,384]{1,0:T(8,128)(2,1)}, bf16[1536,384]{1,0:T(8,128)(2,1)}) custom-call(s32[96]{0:T(128)} %get-tuple-element.241.kt_ref, s32[96]{0:T(128)} %get-tuple-element.242.qt_list_ref, s32[1]{0:T(128)} %get-tuple-element.243.count_ref, bf16[1024,768]{1,0:T(8,128)(2,1)} %copy-done.8, ...), custom_call_target="tpu_custom_call" | custom-call | tf_op jit(solution)/shard_map/attend_back/pallas_call | solution.py:219
  269.4 10.8 %collective-permute-start.15 = (bf16[512,768]{1,0:T(8,128)(2,1)}, bf16[512,768]{1,0:T(8,128)(2,1)}, u32[]{:S(2)}, u32[]{:S(2)}) collective-permute-start(bf16[512,768]{1,0:T(8,128)(2,1)} %constant_dynamic-slice_fusion), channel_id=1, source_target_pairs={{0,1},{1,0},{2,3},{3,2},{4,5},{5,4},{6,7},{7,6},{8,9},{9,8},{10,11... | collective-permute-start | bytes 2359304 | tf_op jit(solution)/shard_map/ppermute | solution.py:753
  286.5 4.4 collective-permute-start.16
  301.4 8.2 %partial_grads.15 = bf16[768,1152]{1,0:T(8,128)(2,1)} custom-call(s32[2]{0:T(128)} %get-tuple-element.390.place_ref, bf16[768,1024]{1,0:T(8,128)(2,1)} %copy-done, bf16[768,1024]{1,0:T(8,128)(2,1)} %copy-done, bf16[768,1024]{1,0:T(8,128)(2,1)} %copy-done, bf16[1024,768]{1,0:T(8,128)(2,1)} %copy-done.18, bf16[1024,768]{1,0:T(8,128)(2,1)} %add_convert_fusion.1.refs_4_, ...), custom_call_target="tpu_custom_call" | custom-call | tf_op jit(solution)/shard_map/partial_grads/pallas_call | solution.py:833
  323.3 3.8 collective-permute-done.22
  329.2 6.5 %partial_grads.16 = bf16[384,1152]{1,0:T(8,128)(2,1)} custom-call(s32[2]{0:T(128)} %pad_add_fusion.2.place_ref, bf16[768,1024]{1,0:T(8,128)(2,1)} %copy-done, bf16[768,1024]{1,0:T(8,128)(2,1)} %copy-done, bf16[768,1024]{1,0:T(8,128)(2,1)} %copy-done, bf16[1024,768]{1,0:T(8,128)(2,1)} %copy-done.18, bf16[1024,768]{1,0:T(8,128)(2,1)} %add_convert_fusion.1.refs_4_, ...), custom_call_target="tpu_custom_call" | custom-call | tf_op jit(solution)/shard_map/partial_grads/pallas_call | solution.py:833
  343.2 6.7 %partial_grads.17.keep_ref = bf16[384,1152]{1,0:T(8,128)(2,1)} custom-call(s32[2]{0:T(128)} %pad_add_fusion.3.place_ref, bf16[768,1024]{1,0:T(8,128)(2,1)} %copy-done, bf16[768,1024]{1,0:T(8,128)(2,1)} %copy-done, bf16[768,1024]{1,0:T(8,128)(2,1)} %copy-done, bf16[1024,768]{1,0:T(8,128)(2,1)} %copy-done.18, bf16[1024,768]{1,0:T(8,128)(2,1)} %add_convert_fusion.1.refs_4_, ...), custom_call_target="tpu_custom_call" | custom-call | tf_op jit(solution)/shard_map/partial_grads/pallas_call | solution.py:833
  350.0 8.7 %collective-permute-done.27 = bf16[48,1920]{1,0:T(8,128)(2,1)S(1)} collective-permute-done((bf16[48,1920]{1,0:T(8,128)(2,1)S(1)}, bf16[48,1920]{1,0:T(8,128)(2,1)S(1)}, u32[]{:S(2)}, u32[]{:S(2)}) %collective-permute-start.27) | collective-permute-done | bytes 184352 | tf_op jit(solution)/shard_map/ppermute | solution.py:979
  374.3 9.5 %collective-permute-done.33.other_ref = bf16[192,1152]{1,0:T(8,128)(2,1)S(1)} collective-permute-done((bf16[192,1152]{1,0:T(8,128)(2,1)}, bf16[192,1152]{1,0:T(8,128)(2,1)S(1)}, u32[]{:S(2)}, u32[]{:S(2)}) %collective-permute-start.33) | collective-permute-done | bytes 442400 | tf_op jit(solution)/shard_map/ppermute | solution.py:764
  395.8 7.1 %assemble.3 = f32[3072,768]{1,0:T(8,128)} custom-call(s32[3]{0:T(128)} %pad_add_fusion.4.place_ref, bf16[16,192,384]{2,1,0:T(8,128)(2,1)} %copy-done.26, bf16[16,192,384]{2,1,0:T(8,128)(2,1)} %collective-permute-done.31.other_ref), custom_call_target="tpu_custom_call" | custom-call | tf_op jit(solution)/shard_map/assemble/pallas_call | solution.py:917
  417.8 3.8 collective-permute-done.44
  426.7 10.8 %assemble.4 = (f32[768,3072]{1,0:T(8,128)}, f32[768,768]{1,0:T(8,128)}) custom-call(s32[3]{0:T(128)} %pad_add_fusion.4.place_ref, bf16[16,48,1920]{2,1,0:T(8,128)(2,1)} %copy-done.21, bf16[16,48,1920]{2,1,0:T(8,128)(2,1)} %collective-permute-done.40.other_ref), custom_call_target="tpu_custom_call" | custom-call | tf_op jit(solution)/shard_map/assemble/pallas_call | solution.py:917
  438.8 12.9 %collective-permute-done.47 = bf16[8,48,1152]{2,1,0:T(8,128)(2,1)S(1)} collective-permute-done((bf16[8,48,1152]{2,1,0:T(8,128)(2,1)S(1)}, bf16[8,48,1152]{2,1,0:T(8,128)(2,1)S(1)}, u32[]{:S(2)}, u32[]{:S(2)}) %collective-permute-start.47) | collective-permute-done | bytes 884768 | tf_op jit(solution)/shard_map/ppermute | solution.py:764
  455.8 7.7 %assemble.5 = (f32[768,768]{1,0:T(8,128)}, f32[768,768]{1,0:T(8,128)}, f32[768,768]{1,0:T(8,128)}) custom-call(s32[3]{0:T(128)} %pad_add_fusion.4.place_ref, bf16[16,48,1152]{2,1,0:T(8,128)(2,1)} %copy-done.27, bf16[16,48,1152]{2,1,0:T(8,128)(2,1)} %collective-permute-done.48.other_ref), custom_call_target="tpu_custom_call" | custom-call | tf_op jit(solution)/shard_map/assemble/pallas_call | solution.py:917
  (281 shorter events, 151.3 us)
Async XLA Ops:
  2.9 18.5 %collective-permute-start = (bf16[512,768]{1,0:T(8,128)(2,1)}, bf16[512,768]{1,0:T(8,128)(2,1)}, u32[]{:S(2)}, u32[]{:S(2)}) collective-permute-start(bf16[512,768]{1,0:T(8,128)(2,1)} %dynamic-slice_bitcast_fusion), channel_id=1, source_target_pairs={{0,1},{1,0},{2,3},{3,2},{4,5},{5,4},{6,7},{7,6},{8,9},{9,8},{10,11... | collective-permute-start | bytes 2359304 | tf_op jit(solution)/shard_map/ppermute | solution.py:753
  129.1 12.0 %collective-permute-start.6 = (bf16[3072,384]{1,0:T(8,128)(2,1)}, bf16[3072,384]{1,0:T(8,128)(2,1)}, u32[]{:S(2)}, u32[]{:S(2)}) collective-permute-start(bf16[3072,384]{1,0:T(8,128)(2,1)} %partial_grads.9), channel_id=1, source_target_pairs={{0,1},{1,0},{2,3},{3,2},{4,5},{5,4},{6,7},{7,6},{8,9},{9,8},{10,11... | collective-permute-start | bytes 7077896 | tf_op jit(solution)/shard_map/ppermute | solution.py:753
  146.4 24.3 %collective-permute-start.7 = (bf16[1536,384]{1,0:T(8,128)(2,1)}, bf16[1536,384]{1,0:T(8,128)(2,1)S(1)}, u32[]{:S(2)}, u32[]{:S(2)}) collective-permute-start(bf16[1536,384]{1,0:T(8,128)(2,1)} %partial_grads.10), channel_id=1, source_target_pairs={{0,2},{1,5},{2,0},{3,7},{4,6},{5,1},{6,4},{7,3},{8,10},{9,13},{10,... | collective-permute-start | bytes 3538952 | tf_op jit(solution)/shard_map/ppermute | solution.py:764
  184.3 27.1 %collective-permute-start.9 = (bf16[768,1920]{1,0:T(8,128)(2,1)}, bf16[768,1920]{1,0:T(8,128)(2,1)}, u32[]{:S(2)}, u32[]{:S(2)}) collective-permute-start(bf16[768,1920]{1,0:T(8,128)(2,1)} %partial_grads.12), channel_id=1, source_target_pairs={{0,1},{1,0},{2,3},{3,2},{4,5},{5,4},{6,7},{7,6},{8,9},{9,8},{10,11... | collective-permute-start | bytes 8847368 | tf_op jit(solution)/shard_map/ppermute | solution.py:753
  185.8 25.5 %collective-permute-start.8 = (bf16[768,384]{1,0:T(8,128)(2,1)S(1)}, bf16[768,384]{1,0:T(8,128)(2,1)S(1)}, u32[]{:S(2)}, u32[]{:S(2)}) collective-permute-start(bf16[768,384]{1,0:T(8,128)(2,1)S(1)} %copy-done.59), channel_id=1, source_target_pairs={{0,4},{1,3},{2,6},{3,1},{4,0},{5,7},{6,2},{7,5},{8,12},{9,11},{10,... | collective-permute-start | bytes 1769480 | tf_op jit(solution)/shard_map/ppermute | solution.py:764
  222.4 38.0 %collective-permute-start.13 = (bf16[384,1920]{1,0:T(8,128)(2,1)}, bf16[384,1920]{1,0:T(8,128)(2,1)S(1)}, u32[]{:S(2)}, u32[]{:S(2)}) collective-permute-start(bf16[384,1920]{1,0:T(8,128)(2,1)} %partial_grads.13), channel_id=1, source_target_pairs={{0,2},{1,5},{2,0},{3,7},{4,6},{5,1},{6,4},{7,3},{8,10},{9,13},{10,... | collective-permute-start | bytes 4423688 | tf_op jit(solution)/shard_map/ppermute | solution.py:764
  224.0 36.4 %collective-permute-start.10 = (bf16[192,384]{1,0:T(8,128)(2,1)}, bf16[192,384]{1,0:T(8,128)(2,1)S(1)}, u32[]{:S(2)}, u32[]{:S(2)}) collective-permute-start(bf16[192,384]{1,0:T(8,128)(2,1)} %get-tuple-element.273), channel_id=1, source_target_pairs={{0,8},{2,10},{4,12},{6,14},{8,0},{10,2},{12,4},{14,6},{16,24},{18,... | collective-permute-start | bytes 442376 | tf_op jit(solution)/shard_map/ppermute | solution.py:979
  224.0 36.4 %collective-permute-start.11 = (bf16[192,384]{1,0:T(8,128)(2,1)}, bf16[192,384]{1,0:T(8,128)(2,1)S(1)}, u32[]{:S(2)}, u32[]{:S(2)}) collective-permute-start(bf16[192,384]{1,0:T(8,128)(2,1)} %get-tuple-element.274), channel_id=1, source_target_pairs={{0,16},{2,18},{4,20},{6,22},{8,24},{10,26},{12,28},{14,30},{16,0},... | collective-permute-start | bytes 442376 | tf_op jit(solution)/shard_map/ppermute | solution.py:979
  228.6 31.8 %collective-permute-start.12 = (bf16[192,384]{1,0:T(8,128)(2,1)}, bf16[192,384]{1,0:T(8,128)(2,1)S(1)}, u32[]{:S(2)}, u32[]{:S(2)}) collective-permute-start(bf16[192,384]{1,0:T(8,128)(2,1)} %get-tuple-element.275), channel_id=1, source_target_pairs={{0,24},{2,26},{4,28},{6,30},{8,16},{10,18},{12,20},{14,22},{16,8},... | collective-permute-start | bytes 442376 | tf_op jit(solution)/shard_map/ppermute | solution.py:979
  269.4 17.2 %collective-permute-start.15 = (bf16[512,768]{1,0:T(8,128)(2,1)}, bf16[512,768]{1,0:T(8,128)(2,1)}, u32[]{:S(2)}, u32[]{:S(2)}) collective-permute-start(bf16[512,768]{1,0:T(8,128)(2,1)} %constant_dynamic-slice_fusion), channel_id=1, source_target_pairs={{0,1},{1,0},{2,3},{3,2},{4,5},{5,4},{6,7},{7,6},{8,9},{9,8},{10,11... | collective-permute-start | bytes 2359304 | tf_op jit(solution)/shard_map/ppermute | solution.py:753
  281.1 12.9 %collective-permute-start.14 = (bf16[512,768]{1,0:T(8,128)(2,1)}, bf16[512,768]{1,0:T(8,128)(2,1)}, u32[]{:S(2)}, u32[]{:S(2)}) collective-permute-start(bf16[512,768]{1,0:T(8,128)(2,1)} %constant_dynamic-slice_fusion.1), channel_id=1, source_target_pairs={{0,1},{1,0},{2,3},{3,2},{4,5},{5,4},{6,7},{7,6},{8,9},{9,8},{10,11... | collective-permute-start | bytes 2359304 | tf_op jit(solution)/shard_map/ppermute | solution.py:753
  281.1 16.0 %collective-permute-start.19 = (bf16[192,1920]{1,0:T(8,128)(2,1)}, bf16[192,1920]{1,0:T(8,128)(2,1)}, u32[]{:S(2)}, u32[]{:S(2)}) collective-permute-start(bf16[192,1920]{1,0:T(8,128)(2,1)} %get-tuple-element.291), channel_id=1, source_target_pairs={{0,4},{1,3},{2,6},{3,1},{4,0},{5,7},{6,2},{7,5},{8,12},{9,11},{10,... | collective-permute-start | bytes 2211848 | tf_op jit(solution)/shard_map/ppermute | solution.py:764
  285.0 12.0 %collective-permute-start.18 = (bf16[192,384]{1,0:T(8,128)(2,1)S(1)}, bf16[192,384]{1,0:T(8,128)(2,1)S(1)}, u32[]{:S(2)}, u32[]{:S(2)}) collective-permute-start(bf16[192,384]{1,0:T(8,128)(2,1)S(1)} %add_convert_fusion.3), channel_id=1, source_target_pairs={{0,24},{2,26},{4,28},{6,30},{8,16},{10,18},{12,20},{14,22},{16,8},... | collective-permute-start | bytes 442376 | tf_op jit(solution)/shard_map/ppermute | solution.py:979
  309.6 17.6 %collective-permute-start.24 = (bf16[768,1152]{1,0:T(8,128)(2,1)}, bf16[768,1152]{1,0:T(8,128)(2,1)}, u32[]{:S(2)}, u32[]{:S(2)}) collective-permute-start(bf16[768,1152]{1,0:T(8,128)(2,1)} %partial_grads.15), channel_id=1, source_target_pairs={{0,1},{1,0},{2,3},{3,2},{4,5},{5,4},{6,7},{7,6},{8,9},{9,8},{10,11... | collective-permute-start | bytes 5308424 | tf_op jit(solution)/shard_map/ppermute | solution.py:753
  309.9 13.4 %collective-permute-start.21 = (bf16[48,1920]{1,0:T(8,128)(2,1)}, bf16[48,1920]{1,0:T(8,128)(2,1)S(1)}, u32[]{:S(2)}, u32[]{:S(2)}) collective-permute-start(bf16[48,1920]{1,0:T(8,128)(2,1)} %get-tuple-element.311), channel_id=1, source_target_pairs={{0,8},{2,10},{4,12},{6,14},{8,0},{10,2},{12,4},{14,6},{16,24},{18,... | collective-permute-start | bytes 552968 | tf_op jit(solution)/shard_map/ppermute | solution.py:979
  310.6 16.5 %collective-permute-start.22 = (bf16[48,1920]{1,0:T(8,128)(2,1)}, bf16[48,1920]{1,0:T(8,128)(2,1)S(1)}, u32[]{:S(2)}, u32[]{:S(2)}) collective-permute-start(bf16[48,1920]{1,0:T(8,128)(2,1)} %get-tuple-element.312), channel_id=1, source_target_pairs={{0,16},{2,18},{4,20},{6,22},{8,24},{10,26},{12,28},{14,30},{16,0},... | collective-permute-start | bytes 552968 | tf_op jit(solution)/shard_map/ppermute | solution.py:979
  312.4 14.7 %collective-permute-start.23 = (bf16[48,1920]{1,0:T(8,128)(2,1)}, bf16[48,1920]{1,0:T(8,128)(2,1)S(1)}, u32[]{:S(2)}, u32[]{:S(2)}) collective-permute-start(bf16[48,1920]{1,0:T(8,128)(2,1)} %get-tuple-element.313), channel_id=1, source_target_pairs={{0,24},{2,26},{4,28},{6,30},{8,16},{10,18},{12,20},{14,22},{16,8},... | collective-permute-start | bytes 552968 | tf_op jit(solution)/shard_map/ppermute | solution.py:979
  314.4 12.8 %collective-permute-start.20 = (bf16[4,192,384]{2,1,0:T(8,128)(2,1)}, bf16[4,192,384]{2,1,0:T(8,128)(2,1)}, u32[]{:S(2)}, u32[]{:S(2)}) collective-permute-start(bf16[4,192,384]{2,1,0:T(8,128)(2,1)} %pad_maximum_fusion.9), channel_id=1, source_target_pairs={{0,4},{1,3},{2,6},{3,1},{4,0},{5,7},{6,2},{7,5},{8,12},{9,11},{10,... | collective-permute-start | bytes 1769480 | tf_op jit(solution)/shard_map/ppermute | solution.py:764
  335.9 25.8 %collective-permute-start.25 = (bf16[8,192,384]{2,1,0:T(8,128)(2,1)S(1)}, bf16[8,192,384]{2,1,0:T(8,128)(2,1)}, u32[]{:S(2)}, u32[]{:S(2)}) collective-permute-start(bf16[8,192,384]{2,1,0:T(8,128)(2,1)S(1)} %pad_maximum_fusion.6), channel_id=1, source_target_pairs={{0,2},{1,5},{2,0},{3,7},{4,6},{5,1},{6,4},{7,3},{8,10},{9,13},{10,... | collective-permute-start | bytes 3538952 | tf_op jit(solution)/shard_map/ppermute | solution.py:764
  336.9 24.7 %collective-permute-start.29 = (bf16[384,1152]{1,0:T(8,128)(2,1)}, bf16[384,1152]{1,0:T(8,128)(2,1)S(1)}, u32[]{:S(2)}, u32[]{:S(2)}) collective-permute-start(bf16[384,1152]{1,0:T(8,128)(2,1)} %partial_grads.16), channel_id=1, source_target_pairs={{0,2},{1,5},{2,0},{3,7},{4,6},{5,1},{6,4},{7,3},{8,10},{9,13},{10,... | collective-permute-start | bytes 2654216 | tf_op jit(solution)/shard_map/ppermute | solution.py:764
  338.0 12.0 %collective-permute-start.28 = (bf16[48,1920]{1,0:T(8,128)(2,1)S(1)}, bf16[48,1920]{1,0:T(8,128)(2,1)S(1)}, u32[]{:S(2)}, u32[]{:S(2)}) collective-permute-start(bf16[48,1920]{1,0:T(8,128)(2,1)S(1)} %add_convert_fusion.2), channel_id=1, source_target_pairs={{0,24},{2,26},{4,28},{6,30},{8,16},{10,18},{12,20},{14,22},{16,8},... | collective-permute-start | bytes 552968 | tf_op jit(solution)/shard_map/ppermute | solution.py:979
  340.2 18.5 %collective-permute-start.27 = (bf16[48,1920]{1,0:T(8,128)(2,1)S(1)}, bf16[48,1920]{1,0:T(8,128)(2,1)S(1)}, u32[]{:S(2)}, u32[]{:S(2)}) collective-permute-start(bf16[48,1920]{1,0:T(8,128)(2,1)S(1)} %add_convert_fusion.2), channel_id=1, source_target_pairs={{0,16},{2,18},{4,20},{6,22},{8,24},{10,26},{12,28},{14,30},{16,0},... | collective-permute-start | bytes 552968 | tf_op jit(solution)/shard_map/ppermute | solution.py:979
  343.2 15.4 %collective-permute-start.26 = (bf16[48,1920]{1,0:T(8,128)(2,1)S(1)}, bf16[48,1920]{1,0:T(8,128)(2,1)S(1)}, u32[]{:S(2)}, u32[]{:S(2)}) collective-permute-start(bf16[48,1920]{1,0:T(8,128)(2,1)S(1)} %add_convert_fusion.2), channel_id=1, source_target_pairs={{0,8},{2,10},{4,12},{6,14},{8,0},{10,2},{12,4},{14,6},{16,24},{18,... | collective-permute-start | bytes 552968 | tf_op jit(solution)/shard_map/ppermute | solution.py:979
  367.4 16.4 %collective-permute-start.31 = (bf16[16,192,384]{2,1,0:T(8,128)(2,1)S(1)}, bf16[16,192,384]{2,1,0:T(8,128)(2,1)}, u32[]{:S(2)}, u32[]{:S(2)}) collective-permute-start(bf16[16,192,384]{2,1,0:T(8,128)(2,1)S(1)} %pad_maximum_fusion.3.own_ref), channel_id=1, source_target_pairs={{0,1},{1,0},{2,3},{3,2},{4,5},{5,4},{6,7},{7,6},{8,9},{9,8},{10,11... | collective-permute-start | bytes 7077896 | tf_op jit(solution)/shard_map/ppermute | solution.py:753
  367.5 16.3 %collective-permute-start.32 = (bf16[4,48,1920]{2,1,0:T(8,128)(2,1)S(1)}, bf16[4,48,1920]{2,1,0:T(8,128)(2,1)S(1)}, u32[]{:S(2)}, u32[]{:S(2)}) collective-permute-start(bf16[4,48,1920]{2,1,0:T(8,128)(2,1)S(1)} %pad_maximum_fusion.8), channel_id=1, source_target_pairs={{0,4},{1,3},{2,6},{3,1},{4,0},{5,7},{6,2},{7,5},{8,12},{9,11},{10,... | collective-permute-start | bytes 2211848 | tf_op jit(solution)/shard_map/ppermute | solution.py:764
  368.6 15.2 %collective-permute-start.33 = (bf16[192,1152]{1,0:T(8,128)(2,1)}, bf16[192,1152]{1,0:T(8,128)(2,1)S(1)}, u32[]{:S(2)}, u32[]{:S(2)}) collective-permute-start(bf16[192,1152]{1,0:T(8,128)(2,1)} %get-tuple-element.336), channel_id=1, source_target_pairs={{0,4},{1,3},{2,6},{3,1},{4,0},{5,7},{6,2},{7,5},{8,12},{9,11},{10,... | collective-permute-start | bytes 1327112 | tf_op jit(solution)/shard_map/ppermute | solution.py:764
  387.4 19.4 %collective-permute-start.35 = (bf16[8,48,1920]{2,1,0:T(8,128)(2,1)S(1)}, bf16[8,48,1920]{2,1,0:T(8,128)(2,1)S(1)}, u32[]{:S(2)}, u32[]{:S(2)}) collective-permute-start(bf16[8,48,1920]{2,1,0:T(8,128)(2,1)S(1)} %pad_maximum_fusion.5), channel_id=1, source_target_pairs={{0,2},{1,5},{2,0},{3,7},{4,6},{5,1},{6,4},{7,3},{8,10},{9,13},{10,... | collective-permute-start | bytes 4423688 | tf_op jit(solution)/shard_map/ppermute | solution.py:764
  388.4 14.5 %collective-permute-start.39 = (f32[12,768]{1,0:T(8,128)S(1)}, f32[12,768]{1,0:T(8,128)S(1)}, u32[]{:S(2)}, u32[]{:S(2)}) collective-permute-start(f32[12,768]{1,0:T(8,128)S(1)} %add.128), channel_id=1, source_target_pairs={{0,4},{2,6},{4,0},{6,2},{8,12},{10,14},{12,8},{14,10},{16,20},{18,... | collective-permute-start | bytes 110600 | tf_op jit(solution)/shard_map/ppermute | solution.py:758
  389.4 13.5 %collective-permute-start.36 = (bf16[48,1152]{1,0:T(8,128)(2,1)}, bf16[48,1152]{1,0:T(8,128)(2,1)S(1)}, u32[]{:S(2)}, u32[]{:S(2)}) collective-permute-start(bf16[48,1152]{1,0:T(8,128)(2,1)} %get-tuple-element.347), channel_id=1, source_target_pairs={{0,8},{2,10},{4,12},{6,14},{8,0},{10,2},{12,4},{14,6},{16,24},{18,... | collective-permute-start | bytes 331784 | tf_op jit(solution)/shard_map/ppermute | solution.py:979
  410.2 14.5 %collective-permute-start.40 = (bf16[16,48,1920]{2,1,0:T(8,128)(2,1)S(1)}, bf16[16,48,1920]{2,1,0:T(8,128)(2,1)}, u32[]{:S(2)}, u32[]{:S(2)}) collective-permute-start(bf16[16,48,1920]{2,1,0:T(8,128)(2,1)S(1)} %pad_maximum_fusion.own_ref), channel_id=1, source_target_pairs={{0,1},{1,0},{2,3},{3,2},{4,5},{5,4},{6,7},{7,6},{8,9},{9,8},{10,11... | collective-permute-start | bytes 8847368 | tf_op jit(solution)/shard_map/ppermute | solution.py:753
  424.7 12.8 %collective-permute-start.45 = (bf16[4,48,1152]{2,1,0:T(8,128)(2,1)S(1)}, bf16[4,48,1152]{2,1,0:T(8,128)(2,1)}, u32[]{:S(2)}, u32[]{:S(2)}) collective-permute-start(bf16[4,48,1152]{2,1,0:T(8,128)(2,1)S(1)} %pad_maximum_fusion.10), channel_id=1, source_target_pairs={{0,4},{1,3},{2,6},{3,1},{4,0},{5,7},{6,2},{7,5},{8,12},{9,11},{10,... | collective-permute-start | bytes 1327112 | tf_op jit(solution)/shard_map/ppermute | solution.py:764
  438.6 13.1 %collective-permute-start.47 = (bf16[8,48,1152]{2,1,0:T(8,128)(2,1)S(1)}, bf16[8,48,1152]{2,1,0:T(8,128)(2,1)S(1)}, u32[]{:S(2)}, u32[]{:S(2)}) collective-permute-start(bf16[8,48,1152]{2,1,0:T(8,128)(2,1)S(1)} %pad_maximum_fusion.7), channel_id=1, source_target_pairs={{0,2},{1,5},{2,0},{3,7},{4,6},{5,1},{6,4},{7,3},{8,10},{9,13},{10,... | collective-permute-start | bytes 2654216 | tf_op jit(solution)/shard_map/ppermute | solution.py:764
  (77 other events, 497.0 us)
